TPU v7x, 256 devices: a whole 4x4x8 slice. The times are simulated.
256 devices in a mesh: mem: 2 (over x_lo), lat: 8 (over y, x_hi), lon: 16 (over z, core).
Axes of the slice: x: 4 (x_hi: 2, x_lo: 2; x = x_hi * 2 + x_lo), y: 4, z: 8, core: 2. Of those that a mesh axis runs over, the one named last changes fastest.
Arguments:
- latent_field: bfloat16 [176, 704, 512], P('lat', 'lon', 'mem'), parts along dimension 2, may hold values from -6 to 6
- norm_gain: float32 [2, 256], replicated, may hold values from 0.1 to 1.9
- mixing: bfloat16 [2, 9, 256, 256], replicated, may hold values from -0.375 to 0.375
- kernel_psi: bfloat16 [2, 9, 176, 3, 45], P(None, None, 'lat'), may hold values from -0.625 to 0.625
- lon_reach: int32 [176], P('lat'), may hold values from 0 to 22, as said below
Outputs:
- latent_out: bfloat16 [176, 704, 512], P('lat', 'lon', 'mem'), parts along dimension 2
There are 2 independent parts, one for each index of `mem`. A program takes and returns all parts, laid end to end along the dimension named above; an argument that names none is the same for every part. Nothing has to cross between parts.
Inputs may be any that keep to these rules, and one draw needn't show every extreme that they name: `lon_reach`: the number of longitude cells on either side that the kernel reaches in each row; the first and the last row reach 22.
All inputs are finite; a program needn't handle non-finite values.
Results may differ from a plain program's by a relative error of at most 0.0056.
Values may be sent and summed in bfloat16 or wider, within the bound.
No kernel may reach another device: no remote copies, remote signals or barrier semaphores. Data moves between devices by JAX's collectives and lax.ppermute only.
A program may use at most 192 MiB of HBM per device.

v0:
```python
import math

import jax
import jax.numpy as jnp
from jax import lax
from jax.sharding import PartitionSpec as P

BLOCKS = 2
HMAX = 22


def with_halo(block, sides, width, periodic):
    for axis, dim in sides:
        count = lax.axis_size(axis)
        forward = [(i, i + 1) for i in range(count - 1)]
        if periodic:
            forward.append((count - 1, 0))
        backward = [(target, source) for source, target in forward]
        low = lax.ppermute(
            lax.slice_in_dim(block, block.shape[dim] - width, None, axis=dim), axis, forward
        )
        high = lax.ppermute(lax.slice_in_dim(block, 0, width, axis=dim), axis, backward)
        block = jnp.concatenate([low, block, high], axis=dim)
    return block


def band_matrix(psi_block, reach_rows, columns, reach_most):
    width = columns + 2 * reach_most
    offset = (
        jnp.arange(width, dtype=jnp.int32)[None, :] - jnp.arange(columns, dtype=jnp.int32)[:, None]
    )
    tap_place = jnp.clip(offset, 0, 2 * reach_most).reshape(-1)
    inside = (offset >= 0) & (offset <= 2 * reach_most)
    allowed = inside[None] & (jnp.abs(offset - reach_most)[None] <= reach_rows[:, None, None])
    taken = jnp.take(psi_block, tap_place, axis=3)
    taken = taken.reshape(psi_block.shape[0], psi_block.shape[1], 3, columns, width)
    zero_value = jnp.zeros((), jnp.bfloat16)
    return jnp.where(allowed[None, :, None], taken, zero_value)


def add_rims(values_in):
    widened = with_halo(values_in, (("lon", 1),), HMAX, True)
    return with_halo(widened, (("lat", 0),), 1, False)


def contract(convolved, band_basis, basis_field):
    rows_here = band_basis.shape[0]
    for shift in range(3):
        convolved = convolved + jnp.einsum(
            "iab,ibc->iac",
            band_basis[:, shift],
            basis_field[shift : shift + rows_here],
            preferred_element_type=jnp.float32,
        )
    return convolved


def local(latent_field, norm_gain, mixing, kernel_psi, lon_reach):
    rows_here, cols_here, chans = latent_field.shape
    basis_count = mixing.shape[1]
    n_lat = rows_here * lax.axis_size("lat")
    n_lon = cols_here * lax.axis_size("lon")
    row_index = (lax.axis_index("lat") * rows_here + jnp.arange(rows_here, dtype=jnp.int32)).astype(
        jnp.float32
    )
    weights = jnp.cos(math.pi * (row_index + 0.5) / n_lat - math.pi / 2)
    all_rows = jnp.arange(n_lat, dtype=jnp.int32).astype(jnp.float32)
    total_weight = n_lon * jnp.sum(jnp.cos(math.pi * (all_rows + 0.5) / n_lat - math.pi / 2))
    current = latent_field
    for layer in range(BLOCKS):
        values = current.astype(jnp.float32)
        weighted = weights[:, None, None]
        sum_first, sum_second = lax.psum(
            (
                jnp.sum(weighted * values, axis=(0, 1)),
                jnp.sum(weighted * values * values, axis=(0, 1)),
            ),
            ("lat", "lon"),
        )
        channel_mean = sum_first / total_weight
        inverse = lax.rsqrt(sum_second / total_weight - channel_mean * channel_mean + 1e-05)
        normed = ((values - channel_mean) * inverse * norm_gain[layer]).astype(jnp.bfloat16)
        band_mats = band_matrix(kernel_psi[layer], lon_reach, cols_here, HMAX)
        mixing_block = mixing[layer]
        start_conv = jnp.zeros((rows_here, cols_here, chans), jnp.float32)
        widened = add_rims(normed)
        flat_rows = widened.reshape(-1, chans)

        def add_input(basis, convolved):
            weight_basis = lax.dynamic_index_in_dim(mixing_block, basis, 0, keepdims=False)
            basis_field = jnp.dot(flat_rows, weight_basis, preferred_element_type=jnp.float32)
            basis_field = basis_field.astype(jnp.bfloat16).reshape(widened.shape)
            band_basis = lax.dynamic_index_in_dim(band_mats, basis, 0, keepdims=False)
            return contract(convolved, band_basis, basis_field)

        convolved = lax.fori_loop(0, basis_count, add_input, start_conv)
        current = (values + jax.nn.gelu(convolved)).astype(jnp.bfloat16)
    return current


def solution(mesh):
    placed = (P("lat", "lon", "mem"), P(), P(), P(None, None, "lat", None, None), P("lat"))
    return jax.shard_map(
        local, mesh=mesh, in_specs=placed, out_specs=P("lat", "lon", "mem"), check_vma=False
    )
```

profile of v0, /device:TPU:1, one launch (start us, length us, event | category | flops | bytes accessed | tf_op | source)
XLA Modules:
  0.0 1157.3 jit_solution(6860124494243217018)
XLA Ops:
  2.8 328.0 %all-reduce.1 = (f32[256]{0:T(256)S(1)}, f32[256]{0:T(256)S(1)}) all-reduce(f32[256]{0:T(256)S(1)} %get-tuple-element.235, f32[256]{0:T(256)S(1)} %get-tuple-element.234), channel_id=1, replica_groups=mesh['mem'=2,'lat'=8,'lon'=16] {'lat','lon'}, use_global_device_ids=true, to_apply=%region_1.0 | all-reduce | flops 512 | bytes 4096 | tf_op jit(solution)/shard_map/psum | solution.py:73
  332.9 7.4 collective-permute-start.1
  341.8 104.2 %gather_fusion = bf16[3872,9,22,3]{2,3,1,0:T(4,128)(2,1)} fusion(bf16[9,22,3,45]{1,2,3,0:T(4,128)(2,1)S(1)} %copy.9, s32[4096]{0:T(1024)S(1)} %pad_clamp_fusion), kind=kCustom, calls=%fused_computation.clone | custom fusion | bytes 9215360 | tf_op jit(solution)/shard_map/jit(_take)/gather | solution.py:35
  446.0 104.4 %gather_fusion.1 = bf16[3872,9,22,3]{2,3,1,0:T(4,128)(2,1)} fusion(bf16[9,22,3,45]{1,2,3,0:T(4,128)(2,1)S(1)} %copy.12, s32[4096]{0:T(1024)S(1)} %pad_clamp_fusion), kind=kCustom, calls=%fused_computation.1.clone | custom fusion | bytes 9215360 | tf_op jit(solution)/shard_map/jit(_take)/gather | solution.py:35
  550.4 46.2 %broadcast_select_fusion.1 = (bf16[3872,9,22,3]{2,3,1,0:T(4,128)(2,1)}, bf16[3872,9,22,3]{2,3,1,0:T(4,128)(2,1)}) fusion(bf16[3872,9,22,3]{2,3,1,0:T(4,128)(2,1)} %gather_fusion, pred[3872]{0:T(1024)(128)(4,1)S(1)} %compare_and_fusion.1, bf16[3872,9,22,3]{2,3,1,0:T(4,128)(2,1)} %gather_fusion.1), kind=kLoop, calls=%fused_computation.27 | loop fusion | flops 4599936 | bytes 18403616 | tf_op jit(solution)/shard_map/jit(_take)/select_n | solution.py:35
  596.5 45.2 %copy.10 = bf16[9,22,3,44,88]{4,3,1,2,0:T(8,128)(2,1)} copy(bf16[9,22,3,44,88]{1,2,0,4,3:T(4,128)(2,1)} %bitcast.117) | data formatting | bytes 9199872 | tf_op jit(solution)/shard_map/reshape | solution.py:36
  641.7 45.2 %copy.13 = bf16[9,22,3,44,88]{4,3,1,2,0:T(8,128)(2,1)} copy(bf16[9,22,3,44,88]{1,2,0,4,3:T(4,128)(2,1)} %bitcast.116) | data formatting | bytes 9199872 | tf_op jit(solution)/shard_map/reshape | solution.py:36
  687.0 11.6 broadcast_select_fusion.3
  699.9 5.5 collective-permute-start.2
  708.1 57.1 %while.28 = (s32[]{:T(128)}, f32[22,44,256]{2,1,0:T(8,128)}, bf16[9,22,3,44,88]{4,3,1,2,0:T(8,128)(2,1)}, bf16[9,256,256]{2,1,0:T(8,128)(2,1)S(1)}, bf16[2112,256]{1,0:T(8,128)(2,1)}, /*index=5*/s32[]{:T(128)}, s32[]{:T(128)}) while((s32[]{:T(128)}, f32[22,44,256]{2,1,0:T(8,128)}, bf16[9,22,3,44,88]{4,3,1,2,0:T(8,128)(2,1)}, ...), condition=%wide.region_6.8_spmd.clone, body=%wide.region_5.7_spmd.clone.sunk | while | flops 409198592 | bytes 32668092 | solution.py:96
  765.2 1.8 fusion.32
  767.0 324.5 %all-reduce = (f32[256]{0:T(256)S(1)}, f32[256]{0:T(256)S(1)}) all-reduce(f32[256]{0:T(256)S(1)} %get-tuple-element.233, f32[256]{0:T(256)S(1)} %get-tuple-element.232), channel_id=1, replica_groups=mesh['mem'=2,'lat'=8,'lon'=16] {'lat','lon'}, use_global_device_ids=true, to_apply=%region_8.10 | all-reduce | flops 512 | bytes 4096 | tf_op jit(solution)/shard_map/psum | solution.py:73
  1093.6 4.4 collective-permute-done.5
  1099.4 5.5 collective-permute-start.6
  1107.4 47.5 %while.29 = (s32[]{:T(128)}, f32[22,44,256]{2,1,0:T(8,128)}, bf16[9,22,3,44,88]{4,3,1,2,0:T(8,128)(2,1)}, bf16[9,256,256]{2,1,0:T(8,128)(2,1)}, bf16[2112,256]{1,0:T(8,128)(2,1)}, /*index=5*/s32[]{:T(128)}, s32[]{:T(128)}) while((s32[]{:T(128)}, f32[22,44,256]{2,1,0:T(8,128)}, bf16[9,22,3,44,88]{4,3,1,2,0:T(8,128)(2,1)}, ...), condition=%wide.region_12.14_spmd.clone, body=%wide.region_11.13_spmd.clone.sunk | while | flops 409198592 | bytes 23230852 | solution.py:96
  1107.4 1.7 fusion.79
  1112.7 1.7 fusion.79
  1118.0 1.7 fusion.79
  1123.2 1.7 fusion.79
  1133.8 1.7 fusion.79
  1139.1 1.7 fusion.79
  1144.3 1.7 fusion.79
  1149.6 1.7 fusion.79
  1154.9 2.4 fusion.33
  (225 shorter events, 105.7 us)
Async XLA Ops:
  331.5 9.0 copy-start.8
  332.9 365.7 %collective-permute-start.1 = (bf16[22,22,256]{2,1,0:T(8,128)(2,1)S(1)}, bf16[22,22,256]{2,1,0:T(8,128)(2,1)S(1)}, u32[]{:S(2)}, u32[]{:S(2)}) collective-permute-start(bf16[22,22,256]{2,1,0:T(8,128)(2,1)S(1)} %get-tuple-element.280), channel_id=1, source_target_pairs={{1,0},{2,1},{3,2},{4,3},{5,4},{6,5},{7,6},{8,7},{9,8},{10,9},{11,1... | collective-permute-start | bytes 743432 | tf_op jit(solution)/shard_map/ppermute | solution.py:22
  340.3 358.3 %collective-permute-start = (bf16[22,22,256]{2,1,0:T(8,128)(2,1)S(1)}, bf16[22,22,256]{2,1,0:T(8,128)(2,1)S(1)}, u32[]{:S(2)}, u32[]{:S(2)}) collective-permute-start(bf16[22,22,256]{2,1,0:T(8,128)(2,1)S(1)} %get-tuple-element.279), channel_id=1, source_target_pairs={{0,1},{1,2},{2,3},{3,4},{4,5},{5,6},{6,7},{7,8},{8,9},{9,10},{10,1... | collective-permute-start | bytes 743432 | tf_op jit(solution)/shard_map/ppermute | solution.py:19
  641.7 45.2 %copy-start.9 = (s32[22]{0:T(128)S(1)}, s32[22]{0:T(128)}, u32[]{:S(2)}) copy-start(s32[22]{0:T(128)} %param.15) | copy-start | bytes 268
  687.0 18.4 %copy-start.7 = (bf16[2,9,256,256]{3,2,1,0:T(8,128)(2,1)S(1)}, bf16[2,9,256,256]{3,2,1,0:T(8,128)(2,1)}, u32[]{:S(2)}) copy-start(bf16[2,9,256,256]{3,2,1,0:T(8,128)(2,1)} %param.13) | copy-start | bytes 7077892
  698.6 8.1 collective-permute-start.3
  699.9 6.8 collective-permute-start.2
  708.1 57.1 %copy-start.2 = (bf16[22,44,256]{2,1,0:T(8,128)(2,1)S(1)}, bf16[22,44,256]{2,1,0:T(8,128)(2,1)}, u32[]{:S(2)}) copy-start(bf16[22,44,256]{2,1,0:T(8,128)(2,1)} %param.11) | copy-start | bytes 1486852
  711.0 1.5 copy-start.1
  717.3 1.5 copy-start.1
  723.6 1.5 copy-start.1
  730.0 1.5 copy-start.1
  736.3 1.5 copy-start.1
  742.7 1.5 copy-start.1
  749.0 1.5 copy-start.1
  755.3 1.5 copy-start.1
  767.0 324.9 %copy-start.3 = (bf16[22,44,256]{2,1,0:T(8,128)(2,1)}, bf16[22,44,256]{2,1,0:T(8,128)(2,1)S(1)}, u32[]{:S(2)}) copy-start(bf16[22,44,256]{2,1,0:T(8,128)(2,1)S(1)} %get-tuple-element.262) | copy-start | bytes 1486852
  1091.9 6.2 collective-permute-start.5
  1093.0 5.0 collective-permute-start.4
  1098.1 6.8 collective-permute-start.7
  1099.4 6.6 collective-permute-start.6
  1107.4 47.5 %copy-start.4 = (bf16[22,44,256]{2,1,0:T(8,128)(2,1)S(1)}, bf16[22,44,256]{2,1,0:T(8,128)(2,1)}, u32[]{:S(2)}) copy-start(bf16[22,44,256]{2,1,0:T(8,128)(2,1)} %copy-done.3) | copy-start | bytes 1486852
  1114.6 1.5 copy-start
  1119.9 1.5 copy-start
  (26 other events, 33.1 us)
where the time goes:
time: 1160 us
  blocking collectives  653 us (56%)
  local copies, waits for them, and re-layouts  342 us (29%)
  other arithmetic  68.5 us (6%)
  matrix products  64.4 us (6%)
  starting transfers between devices  22.8 us (2%)
    psum x2, blocking collectives, local(): lax.psum((jnp.sum(weighted * values, axis=(0, 1)), jnp.sum(weighted * val...  653 us
    gather x2, local copies, waits for them, and re-layouts, band_matrix(): taken = jnp.take(psi_block, tap_place, axis=3)  209 us
    reshape x2, local copies, waits for them, and re-layouts, band_matrix(): taken.reshape(psi_block.shape[0], psi_block.shape[1], 3, columns, width)  90.3 us
    select_n x2, other arithmetic, band_matrix(): taken = jnp.take(psi_block, tap_place, axis=3)  46.2 us
    dot_general x54, matrix products, contract(): jnp.einsum('iab,ibc->iac', band_basis[:, shift], basis_field[shift:shift...  34.2 us
    dot_general x18, matrix products, add_input(): jnp.dot(flat_rows, weight_basis, preferred_element_type=jnp.float32)  30.2 us
    squeeze x18, local copies, waits for them, and re-layouts, add_input(): band_basis = lax.dynamic_index_in_dim(band_mats, basis, 0, keepdims=False)  23.2 us
  transfers between devices with their start and end apart: 8, of which 2 were waited for; matrix products, arithmetic and copies ran while one was open for 31% of the time, Pallas kernels for 0%

commit v1 on v0

v1 whole, which is shorter than its diff:
```python
import functools
import math

import jax
import jax.numpy as jnp
from jax import lax
from jax.experimental import pallas as pl
from jax.experimental.pallas import tpu as pltpu
from jax.sharding import Mesh, PartitionSpec as P

BLOCKS = 2
HMAX = 22
TAPS = 2 * HMAX + 1
TILE = 16
SPAN = 64
LAT = ("y", "xh")
LON = ("z", "core")
F32 = jnp.float32
BF16 = jnp.bfloat16
VMEM_LIMIT = 56 * 1024 * 1024


def area_weight(row, n_lat):
    return jnp.cos(math.pi * (row.astype(F32) + 0.5) / n_lat - math.pi / 2)


def sums_kernel(x_ref, w_ref, out_ref):
    rows, _, chans = x_ref.shape

    def add_row(i, carry):
        first, second = carry
        v = x_ref[i].astype(F32)
        w = w_ref[i]
        return (
            first + w * jnp.sum(v, axis=0, keepdims=True),
            second + w * jnp.sum(v * v, axis=0, keepdims=True),
        )

    zero = jnp.zeros((1, chans), F32)
    first, second = lax.fori_loop(0, rows, add_row, (zero, zero))
    out_ref[0:1] = first
    out_ref[1:2] = second


def band_kernel(taps_ref, band_ref):
    pairs, _, basis, _ = taps_ref.shape

    def one_pair(p, _):
        for ri in range(2):
            for k in range(basis):
                for half in range(2):
                    lanes = slice(128 * half, 128 * half + 128)
                    line = taps_ref[p, ri, k : k + 1, lanes]
                    spread = jnp.broadcast_to(line, (TILE, 128))
                    moved = pltpu.roll(spread, 0, 1, stride=1, stride_axis=0)
                    at = (ri * basis + k) * TILE
                    band_ref[p, at : at + TILE, lanes] = moved.astype(BF16)
        return 0

    lax.fori_loop(0, pairs, one_pair, 0)


def gain_of(gathered_ref, gain_ref, total_weight):
    total = jnp.sum(gathered_ref[...], axis=0)
    mean = total[0:1] / total_weight
    inverse = lax.rsqrt(total[1:2] / total_weight - mean * mean + 1e-05)
    return mean, inverse, gain_ref[...]


def convolve(u_ref, band_ref, s_ref, rows, cols):
    basis = band_ref.shape[1] // (2 * TILE)
    chans = u_ref.shape[2]
    tiles = cols // TILE

    def one_pair(p, _):
        band = band_ref[p]
        for t in range(tiles):
            window = u_ref[pl.ds(2 * p, 4), TILE * t : TILE * t + SPAN, :]
            window = window.reshape(4 * SPAN, chans)
            s = jnp.dot(band, window, preferred_element_type=F32).astype(BF16)
            for ri in range(2):
                for k in range(basis):
                    at = (ri * basis + k) * TILE
                    s_ref[2 * p + ri, TILE * t : TILE * t + TILE, k * chans : (k + 1) * chans] = s[
                        at : at + TILE
                    ]
        return 0

    lax.fori_loop(0, rows // 2, one_pair, 0)


def first_kernel(
    n_lat, n_lon, place_ref, w_ref, left_right_z, own_ref, left_right_core, gathered_ref, gain_ref,
    band_ref, mix_ref, out_ref, sums_ref, u_ref, res_ref, s_ref,
):
    rows_in, width, chans = own_ref.shape
    rows, cols, _ = out_ref.shape
    total_weight = w_ref[rows]
    mean, inverse, gain = gain_of(gathered_ref, gain_ref, total_weight)
    core = place_ref[1]
    top = place_ref[0]

    def one_row(r, _):
        from_z = left_right_z[r].astype(F32)
        from_core = left_right_core[r].astype(F32)
        own = own_ref[r].astype(F32)
        left = jnp.where(core == 0, from_z, from_core)
        right = jnp.where(core == 0, from_core, from_z)
        pad = jnp.zeros((u_ref.shape[1] - 3 * width, chans), F32)
        full = jnp.concatenate([left, own, right, pad], axis=0)
        here = top + r
        inside = (here >= 0) & (here < n_lat)
        u = jnp.where(inside, (full - mean) * inverse * gain, 0.0)
        u_ref[r] = u.astype(BF16)
        res = jnp.concatenate([left[HMAX:], own, right[:HMAX], pad[: cols - 2 * width]], axis=0)
        res_ref[r] = res.astype(BF16)
        return 0

    lax.fori_loop(0, rows_in, one_row, 0)
    convolve(u_ref, band_ref, s_ref, rows, cols)
    column = lax.broadcasted_iota(jnp.int32, (cols, chans), 0)
    mine = (column >= HMAX) & (column < HMAX + width)
    group = 3

    def mix_rows(g, carry):
        first, second = carry
        lhs = s_ref[pl.ds(group * g, group)].reshape(group * cols, s_ref.shape[2])
        conv = jnp.dot(lhs, mix_ref[...], preferred_element_type=F32)
        grown = jax.nn.gelu(conv).reshape(group, cols, chans)
        for n in range(group):
            i = group * g + n
            new = (res_ref[i + 1].astype(F32) + grown[n]).astype(BF16)
            out_ref[i] = new
            v = jnp.where(mine, new.astype(F32), 0.0)
            w = w_ref[i]
            first = first + w * jnp.sum(v, axis=0, keepdims=True)
            second = second + w * jnp.sum(v * v, axis=0, keepdims=True)
        return first, second

    zero = jnp.zeros((1, chans), F32)
    first, second = lax.fori_loop(0, rows // group, mix_rows, (zero, zero))
    sums_ref[0:1] = first
    sums_ref[1:2] = second


def second_kernel(
    n_lat, n_lon, place_ref, w_ref, x_ref, gathered_ref, gain_ref, band_ref, mix_ref, out_ref,
    u_ref, s_ref,
):
    rows_in, wide, chans = x_ref.shape
    rows, cols, _ = out_ref.shape
    cols_pad = s_ref.shape[1]
    total_weight = w_ref[rows_in]
    mean, inverse, gain = gain_of(gathered_ref, gain_ref, total_weight)
    top = place_ref[0] + 1

    def one_row(r, _):
        here = top + r
        inside = (here >= 0) & (here < n_lat)
        u = jnp.where(inside, (x_ref[r].astype(F32) - mean) * inverse * gain, 0.0)
        u_ref[r] = u.astype(BF16)
        return 0

    lax.fori_loop(0, rows_in, one_row, 0)
    convolve(u_ref, band_ref, s_ref, rows, cols_pad)
    group = 11

    def mix_rows(g, _):
        lhs = s_ref[pl.ds(group * g, group)].reshape(group * cols_pad, s_ref.shape[2])
        conv = jnp.dot(lhs, mix_ref[...], preferred_element_type=F32)
        grown = jax.nn.gelu(conv).reshape(group, cols_pad, chans)
        for n in range(group):
            i = group * g + n
            res = x_ref[i + 1].astype(F32)[HMAX : HMAX + cols]
            out_ref[i] = (res + grown[n, :cols]).astype(BF16)
        return 0

    lax.fori_loop(0, rows // group, mix_rows, 0)


def vmem():
    return pl.BlockSpec(memory_space=pltpu.VMEM)


def smem():
    return pl.BlockSpec(memory_space=pltpu.SMEM)


def call(kernel, out_shape, ins, scratch=(), flops=0, moved=0):
    return pl.pallas_call(
        kernel,
        out_shape=out_shape,
        in_specs=[smem() if s else vmem() for s in ins],
        out_specs=jax.tree.map(lambda _: vmem(), out_shape),
        scratch_shapes=list(scratch),
        compiler_params=pltpu.CompilerParams(vmem_limit_bytes=VMEM_LIMIT),
        cost_estimate=pl.CostEstimate(flops=flops, bytes_accessed=moved, transcendentals=0),
    )


def swap_pairs(count, first):
    pairs = []
    for i in range(first, count - 1, 2):
        pairs += [(i, i + 1), (i + 1, i)]
    return pairs


def spread_taps(masked):
    basis, rows, _, _ = masked.shape
    lines = jnp.pad(masked.astype(F32), ((0, 0), (0, 0), (0, 0), (0, SPAN - TAPS)))
    lines = lines.reshape(basis, rows // 2, 2, 3 * SPAN)
    even = jnp.pad(lines[:, :, 0], ((0, 0), (0, 0), (0, SPAN)))
    odd = jnp.pad(lines[:, :, 1], ((0, 0), (0, 0), (SPAN, 0)))
    return jnp.transpose(jnp.stack([even, odd], axis=2), (1, 2, 0, 3))


def bands_of(masked):
    taps = spread_taps(masked)
    pairs, _, basis, _ = taps.shape
    shape = jax.ShapeDtypeStruct((pairs, 2 * basis * TILE, 4 * SPAN), BF16)
    return call(band_kernel, shape, [False], flops=10**6, moved=4 * 10**6)(taps)


def gather_sums(sums):
    sums = sums + lax.ppermute(sums, "core", [(0, 1), (1, 0)])
    axes = ("y", "xh", "z")
    count = math.prod(lax.axis_size(a) for a in axes)
    return lax.all_to_all(jnp.broadcast_to(sums[None], (count,) + sums.shape), axes, 0, 0)


def local(x, norm_gain, mixing, kernel_psi, lon_reach):
    rows, cols, chans = x.shape
    basis = mixing.shape[1]
    n_lat = rows * lax.axis_size("y") * lax.axis_size("xh")
    n_lon = cols * lax.axis_size("z") * lax.axis_size("core")
    lat = lax.axis_index("y") * 2 + lax.axis_index("xh")
    xh = lax.axis_index("xh")
    core = lax.axis_index("core")
    top = lat * rows
    all_weights = area_weight(jnp.arange(n_lat, dtype=jnp.int32), n_lat)
    total_weight = n_lon * jnp.sum(all_weights)
    own_rows = top + jnp.arange(rows, dtype=jnp.int32)
    weights = area_weight(own_rows, n_lat)
    zero = jnp.zeros((1,), F32)
    wide_weights = jnp.concatenate([zero, weights, zero, total_weight[None]])
    place = jnp.stack([top - 2, core]).astype(jnp.int32)

    tap = jnp.arange(TAPS, dtype=jnp.int32) - HMAX
    keep = jnp.abs(tap)[None] <= lon_reach[:, None]
    masked = jnp.where(keep[None, None, :, None, :], kernel_psi, jnp.zeros((), BF16))

    def lat_message(edge_rows, tap_row):
        flat = tap_row.reshape(-1)
        count = -(-flat.shape[0] // chans)
        flat = jnp.pad(flat, (0, count * chans - flat.shape[0])).reshape(count, chans)
        return jnp.concatenate([edge_rows.reshape(-1, chans), flat], axis=0)

    low = lat_message(x[:2], masked[0, :, 0])
    high = lat_message(x[rows - 2 :], masked[0, :, rows - 1])
    got_a = lax.ppermute(jnp.where(xh == 0, high, low), LAT, swap_pairs(8, 0))
    got_b = lax.ppermute(jnp.where(xh == 0, low, high), LAT, swap_pairs(8, 1))
    above = jnp.where(xh == 0, got_b, got_a)
    below = jnp.where(xh == 0, got_a, got_b)

    def taps_from(message):
        return message[2 * cols :].reshape(-1)[: basis * 3 * TAPS].reshape(basis, 1, 3, TAPS)

    tall = jnp.concatenate(
        [above[: 2 * cols].reshape(2, cols, chans), x, below[: 2 * cols].reshape(2, cols, chans)],
        axis=0,
    )
    from_core = lax.ppermute(tall, "core", [(0, 1), (1, 0)])
    ring = []
    for z in range(8):
        a, b = 2 * z + 1, (2 * z + 2) % 16
        ring += [(a, b), (b, a)]
    from_z = lax.ppermute(tall, LON, ring)

    sums_shape = jax.ShapeDtypeStruct((2, chans), F32)
    sums = call(sums_kernel, sums_shape, [False, True], moved=10**6, flops=10**6)(x, weights)
    gathered = gather_sums(sums)

    bands_second = bands_of(masked[1])
    bands_first = bands_of(jnp.concatenate([taps_from(above), masked[0], taps_from(below)], axis=1))

    wide = 96
    tall_rows = rows + 4
    deep = basis * chans
    x1, sums1 = call(
        functools.partial(first_kernel, n_lat, n_lon),
        (jax.ShapeDtypeStruct((rows + 2, wide, chans), BF16), sums_shape),
        [True, True] + [False] * 7,
        [
            pltpu.VMEM((tall_rows, 144, chans), BF16),
            pltpu.VMEM((tall_rows, wide, chans), BF16),
            pltpu.VMEM((rows + 2, wide, deep), BF16),
        ],
        flops=5 * 10**9,
        moved=10**7,
    )(
        place, wide_weights, from_z, tall, from_core, gathered, norm_gain[0:1], bands_first,
        mixing[0].reshape(deep, chans),
    )
    gathered1 = gather_sums(sums1)
    return call(
        functools.partial(second_kernel, n_lat, n_lon),
        jax.ShapeDtypeStruct((rows, cols, chans), BF16),
        [True, True] + [False] * 5,
        [pltpu.VMEM((rows + 2, wide, chans), BF16), pltpu.VMEM((rows, 48, deep), BF16)],
        flops=25 * 10**8,
        moved=5 * 10**6,
    )(
        place, wide_weights, x1, gathered1, norm_gain[1:2], bands_second,
        mixing[1].reshape(deep, chans),
    )


def solution(mesh):
    split = Mesh(mesh.devices.reshape(2, 4, 2, 8, 2), ("mem", "y", "xh", "z", "core"))
    placed = (P(LAT, LON, "mem"), P(), P(), P(None, None, LAT, None, None), P(LAT))
    return jax.shard_map(
        local, mesh=split, in_specs=placed, out_specs=P(LAT, LON, "mem"), check_vma=False
    )
```

time: 1160 us -> 96.9 us (0.08)
  blocking collectives: 653 us -> 0 us
  local copies, waits for them, and re-layouts: 342 us -> 8.32 us
  matrix products: 64.4 us -> 0 us
  other arithmetic: 68.5 us -> 6.83 us
  Pallas kernels: 0 us -> 32.1 us
  starting transfers between devices: 22.8 us -> 36.3 us
    psum x2 -> x0, blocking collectives: 653 us -> none  [local(): lax.psum((jnp.sum(weighted * values, axis=(0, 1)), jnp.sum(weighted * val...]
    gather x2 -> x0, local copies, waits for them, and re-layouts: 209 us -> none  [band_matrix(): taken = jnp.take(psi_block, tap_place, axis=3)]
    reshape x2 -> x14, local copies, waits for them, and re-layouts: 90.3 us -> 1.12 us  [the longest x4 0.81 us: spread_taps(): lines = lines.reshape(basis, rows // 2, 2, 3 * SPAN)]
    dot_general x72 -> x0, matrix products: 64.4 us -> none  [the longest x54 34.2 us: contract(): jnp.einsum('iab,ibc->iac', band_basis[:, shift], basis_field[shift:shift...]
    select_n x3, other arithmetic: 57.7 us -> 1.19 us  [the longest x1 1.16 us: local(): jnp.where(keep[None, None, :, None, :], kernel_psi, jnp.zeros((), BF16))]
    pallas_call x0 -> x5, Pallas kernels: none -> 32.1 us  [the longest x1 14.5 us: local(): call(functools.partial(first_kernel, n_lat, n_lon), (jax.ShapeDtypeStruct...]
    squeeze x22 -> x1, local copies, waits for them, and re-layouts: 25.3 us -> 0.03 us  [spread_taps(): odd = jnp.pad(lines[:, :, 1], ((0, 0), (0, 0), (SPAN, 0)))]
    all_to_all x0 -> x2, starting transfers between devices: none -> 23.3 us  [gather_sums(): lax.all_to_all(jnp.broadcast_to(sums[None], (count,) + sums.shape), axes,...]
  transfers between devices with their start and end apart: 8 -> 8, of which waited for: 2 -> 3; matrix products, arithmetic and copies ran while one was open for 31% -> 9% of each run, Pallas kernels for 0% -> 9%
where the time goes in v1:
time: 96.9 us; the launch traced here: 96.5 us
  starting transfers between devices  36.3 us (37%)
  Pallas kernels  32.1 us (33%)
  waiting for transfers between devices  11.9 us (12%)
  local copies, waits for them, and re-layouts  8.32 us (9%)
  other arithmetic  6.83 us (7%)
  between operations  1.04 us (1%)
    all_to_all x2, starting transfers between devices, gather_sums(): lax.all_to_all(jnp.broadcast_to(sums[None], (count,) + sums.shape), axes,...  23.3 us
    pallas_call x1, Pallas kernels, local(): call(functools.partial(first_kernel, n_lat, n_lon), (jax.ShapeDtypeStruct...  14.5 us
    all_to_all x2, waiting for transfers between devices, gather_sums(): lax.all_to_all(jnp.broadcast_to(sums[None], (count,) + sums.shape), axes,...  10.9 us
    pallas_call x1, Pallas kernels, local(): call(functools.partial(second_kernel, n_lat, n_lon), jax.ShapeDtypeStruct...  8.69 us
    pallas_call x2, Pallas kernels, bands_of(): call(band_kernel, shape, [False], flops=10 ** 6, moved=4 * 10 ** 6)(taps)  6.89 us
    ppermute x1, starting transfers between devices, local(): got_a = lax.ppermute(jnp.where(xh == 0, high, low), LAT, swap_pairs(8, 0))  6.14 us
    ppermute x2, starting transfers between devices, gather_sums(): sums = sums + lax.ppermute(sums, 'core', [(0, 1), (1, 0)])  3.42 us
    pallas_call x1, Pallas kernels, local(): call(sums_kernel, sums_shape, [False, True], moved=10 ** 6, flops=10 ** 6)  2.08 us
  transfers between devices with their start and end apart: 8, of which 3 were waited for; matrix products, arithmetic and copies ran while one was open for 9% of the time, Pallas kernels for 9%

profile of v1, /device:TPU:1, one launch (start us, length us, event | category | flops | bytes accessed | tf_op | source)
XLA Modules:
  0.0 96.5 jit_solution(5477223864452870960)
XLA Ops:
  0.0 0.7 broadcast_compare_fusion
  0.7 1.2 %copy_select_fusion = bf16[2,9,22,3,45]{4,2,3,1,0:T(8,128)(2,1)S(1)} fusion(bf16[2,9,22,3,45]{4,0,3,2,1:T(2,128)(2,1)} %param.8, pred[22,45]{1,0:T(8,128)(4,1)S(1)} %broadcast_compare_fusion), kind=kLoop, calls=%fused_computation.6 | loop fusion | flops 53460 | bytes 214830 | tf_op jit(solution)/shard_map/jit(_where)/select_n | solution.py:250
  2.3 0.8 fusion.7
  3.9 6.1 %collective-permute-start.1 = (bf16[93,256]{1,0:T(8,128)(2,1)S(1)}, bf16[93,256]{1,0:T(8,128)(2,1)S(1)}, u32[]{:S(2)}, u32[]{:S(2)}) collective-permute-start(bf16[93,256]{1,0:T(8,128)(2,1)S(1)} %get-tuple-element.23), channel_id=1, source_target_pairs={{0,16},{16,0},{32,48},{48,32},{64,80},{80,64},{96,112},{112,96},{1... | collective-permute-start | bytes 142856 | tf_op jit(solution)/shard_map/ppermute | solution.py:260
  10.7 2.1 %shard_map.55 = f32[2,256]{1,0:T(2,128)} custom-call(bf16[22,44,256]{2,1,0:T(8,128)(2,1)} %x_ref.1, f32[22]{0:T(128)} %add_cosine_fusion.w_ref), custom_call_target="tpu_custom_call" | custom-call | flops 1000000 | bytes 1000000 | tf_op jit(solution)/shard_map/pallas_call | solution.py:280
  12.7 1.2 %collective-permute-start.4 = (f32[2,256]{1,0:T(2,128)}, f32[2,256]{1,0:T(2,128)S(1)}, u32[]{:S(2)}, u32[]{:S(2)}) collective-permute-start(f32[2,256]{1,0:T(2,128)} %shard_map.55), channel_id=1, source_target_pairs={{0,1},{1,0},{2,3},{3,2},{4,5},{5,4},{6,7},{7,6},{8,9},{9,8},{10,11... | collective-permute-start | bytes 6152 | tf_op jit(solution)/shard_map/ppermute | solution.py:225
  14.7 1.6 %fusion.6 = (bf16[1,9,256,256]{3,2,1,0:T(8,128)(2,1)}, bf16[1,9,256,256]{3,2,1,0:T(8,128)(2,1)}) fusion(bf16[2,9,256,256]{3,2,1,0:T(8,128)(2,1)S(1)} %copy-done.1), kind=kLoop, calls=%fused_computation.40 | loop fusion | bytes 4718592 | tf_op jit(solution)/shard_map/slice | solution.py:314
  19.3 0.7 broadcast_in_dim.33
  20.0 13.3 %all-to-all-start = ((f32[64,2,256]{2,1,0:T(2,128)}), f32[64,2,256]{2,1,0:T(2,128)S(1)}, u32[]{:S(2)}, u32[]{:S(2)}) async-start(f32[64,2,256]{2,1,0:T(2,128)} %broadcast_in_dim.33), calls=%async_computation | async-start | bytes 262144 | tf_op jit(solution)/shard_map/all_to_all | solution.py:228
  33.5 1.5 %collective-permute-start.2 = (bf16[26,44,256]{2,1,0:T(8,128)(2,1)S(1)}, bf16[26,44,256]{2,1,0:T(8,128)(2,1)S(1)}, u32[]{:S(2)}, u32[]{:S(2)}) collective-permute-start(bf16[26,44,256]{2,1,0:T(8,128)(2,1)S(1)} %constant_dynamic-update-slice_fusion.4.own_ref), channel_id=1, source_target_pairs={{1,2},{2,1},{3,4},{4,3},{5,6},{6,5},{7,8},{8,7},{9,10},{10,9},{11,... | collective-permute-start | bytes 1757192 | tf_op jit(solution)/shard_map/ppermute | solution.py:277
  35.1 1.2 %collective-permute-start.3 = (bf16[26,44,256]{2,1,0:T(8,128)(2,1)S(1)}, bf16[26,44,256]{2,1,0:T(8,128)(2,1)S(1)}, u32[]{:S(2)}, u32[]{:S(2)}) collective-permute-start(bf16[26,44,256]{2,1,0:T(8,128)(2,1)S(1)} %constant_dynamic-update-slice_fusion.4.own_ref), channel_id=1, source_target_pairs={{0,1},{1,0},{2,3},{3,2},{4,5},{5,4},{6,7},{7,6},{8,9},{9,8},{10,11... | collective-permute-start | bytes 1757192 | tf_op jit(solution)/shard_map/ppermute | solution.py:272
  37.5 0.8 maximum_bitcast_fusion.taps_ref
  38.3 3.5 %shard_map.56.band_ref = bf16[12,288,256]{2,1,0:T(8,128)(2,1)} custom-call(f32[12,2,9,256]{3,2,1,0:T(8,128)} %maximum_bitcast_fusion.taps_ref), custom_call_target="tpu_custom_call" | custom-call | flops 1000000 | bytes 4000000 | tf_op jit(solution)/shard_map/pallas_call | solution.py:221
  41.8 3.4 %all-to-all-done.gathered_ref = f32[64,2,256]{2,1,0:T(2,128)S(1)} async-done(((f32[64,2,256]{2,1,0:T(2,128)}), f32[64,2,256]{2,1,0:T(2,128)S(1)}, u32[]{:S(2)}, u32[]{:S(2)}) %all-to-all-start) | async-done | bytes 131104 | tf_op jit(solution)/shard_map/all_to_all | solution.py:228
  46.2 14.5 %shard_map.57 = (bf16[24,96,256]{2,1,0:T(8,128)(2,1)}, f32[2,256]{1,0:T(2,128)}) custom-call(s32[2]{0:T(128)} %pad_add_fusion.place_ref, f32[25]{0:T(128)} %pad_maximum_fusion.w_ref, bf16[26,44,256]{2,1,0:T(8,128)(2,1)} %copy-done.8, bf16[26,44,256]{2,1,0:T(8,128)(2,1)} %copy-done.5, bf16[26,44,256]{2,1,0:T(8,128)(2,1)} %copy-done.9, ...), custom_call_target="tpu_custom_call" | custom-call | flops 5000000000 | bytes 10000000 | tf_op jit(solution)/shard_map/pallas_call | solution.py:289
  60.7 2.2 %collective-permute-start.5 = (f32[2,256]{1,0:T(2,128)}, f32[2,256]{1,0:T(2,128)S(1)}, u32[]{:S(2)}, u32[]{:S(2)}) collective-permute-start(f32[2,256]{1,0:T(2,128)} %get-tuple-element.8), channel_id=1, source_target_pairs={{0,1},{1,0},{2,3},{3,2},{4,5},{5,4},{6,7},{7,6},{8,9},{9,8},{10,11... | collective-permute-start | bytes 6152 | tf_op jit(solution)/shard_map/ppermute | solution.py:225
  62.9 1.0 %collective-permute-done.5 = f32[2,256]{1,0:T(2,128)S(1)} collective-permute-done((f32[2,256]{1,0:T(2,128)}, f32[2,256]{1,0:T(2,128)S(1)}, u32[]{:S(2)}, u32[]{:S(2)}) %collective-permute-start.5) | collective-permute-done | bytes 2080 | tf_op jit(solution)/shard_map/ppermute | solution.py:225
  63.9 0.7 add.55
  64.6 0.7 broadcast_in_dim.34
  65.3 10.1 %all-to-all-start.1 = ((f32[64,2,256]{2,1,0:T(2,128)}), f32[64,2,256]{2,1,0:T(2,128)S(1)}, u32[]{:S(2)}, u32[]{:S(2)}) async-start(f32[64,2,256]{2,1,0:T(2,128)} %broadcast_in_dim.34), calls=%async_computation.1 | async-start | bytes 262144 | tf_op jit(solution)/shard_map/all_to_all | solution.py:228
  75.5 0.8 maximum_bitcast_fusion.1.taps_ref
  76.3 3.4 %shard_map.58.band_ref = bf16[11,288,256]{2,1,0:T(8,128)(2,1)} custom-call(f32[11,2,9,256]{3,2,1,0:T(8,128)} %maximum_bitcast_fusion.1.taps_ref), custom_call_target="tpu_custom_call" | custom-call | flops 1000000 | bytes 4000000 | tf_op jit(solution)/shard_map/pallas_call | solution.py:221
  79.6 7.5 %all-to-all-done.1.gathered_ref = f32[64,2,256]{2,1,0:T(2,128)S(1)} async-done(((f32[64,2,256]{2,1,0:T(2,128)}), f32[64,2,256]{2,1,0:T(2,128)S(1)}, u32[]{:S(2)}, u32[]{:S(2)}) %all-to-all-start.1) | async-done | bytes 131104 | tf_op jit(solution)/shard_map/all_to_all | solution.py:228
  87.8 8.7 %shard_map.59 = bf16[22,44,256]{2,1,0:T(8,128)(2,1)} custom-call(s32[2]{0:T(128)} %pad_add_fusion.place_ref, f32[25]{0:T(128)} %pad_maximum_fusion.w_ref, bf16[24,96,256]{2,1,0:T(8,128)(2,1)} %get-tuple-element.7.x_ref, f32[64,2,256]{2,1,0:T(2,128)} %copy-done.3, f32[1,256]{1,0:T(1,128)} %get-tuple-element.25.gain_ref, ...), custom_call_target="tpu_custom_call" | custom-call | flops 2500000000 | bytes 5000000 | tf_op jit(solution)/shard_map/pallas_call | solution.py:305
  (76 shorter events, 7.9 us)
Async XLA Ops:
  0.7 13.9 %copy-start.1 = (bf16[2,9,256,256]{3,2,1,0:T(8,128)(2,1)S(1)}, bf16[2,9,256,256]{3,2,1,0:T(8,128)(2,1)}, u32[]{:S(2)}) copy-start(bf16[2,9,256,256]{3,2,1,0:T(8,128)(2,1)} %param.7) | copy-start | bytes 7077892
  3.2 30.1 %collective-permute-start = (bf16[93,256]{1,0:T(8,128)(2,1)S(1)}, bf16[93,256]{1,0:T(8,128)(2,1)S(1)}, u32[]{:S(2)}, u32[]{:S(2)}) collective-permute-start(bf16[93,256]{1,0:T(8,128)(2,1)S(1)} %get-tuple-element.24), channel_id=1, source_target_pairs={{16,32},{32,16},{48,64},{64,48},{80,96},{96,80},{17,33},{33,17},{4... | collective-permute-start | bytes 142856 | tf_op jit(solution)/shard_map/ppermute | solution.py:261
  3.9 29.4 %collective-permute-start.1 = (bf16[93,256]{1,0:T(8,128)(2,1)S(1)}, bf16[93,256]{1,0:T(8,128)(2,1)S(1)}, u32[]{:S(2)}, u32[]{:S(2)}) collective-permute-start(bf16[93,256]{1,0:T(8,128)(2,1)S(1)} %get-tuple-element.23), channel_id=1, source_target_pairs={{0,16},{16,0},{32,48},{48,32},{64,80},{80,64},{96,112},{112,96},{1... | collective-permute-start | bytes 142856 | tf_op jit(solution)/shard_map/ppermute | solution.py:260
  12.7 6.6 %collective-permute-start.4 = (f32[2,256]{1,0:T(2,128)}, f32[2,256]{1,0:T(2,128)S(1)}, u32[]{:S(2)}, u32[]{:S(2)}) collective-permute-start(f32[2,256]{1,0:T(2,128)} %shard_map.55), channel_id=1, source_target_pairs={{0,1},{1,0},{2,3},{3,2},{4,5},{5,4},{6,7},{7,6},{8,9},{9,8},{10,11... | collective-permute-start | bytes 6152 | tf_op jit(solution)/shard_map/ppermute | solution.py:225
  14.7 1.6 %copy-start.7 = (f32[2,256]{1,0:T(2,128)S(1)}, f32[2,256]{1,0:T(2,128)}, u32[]{:S(2)}) copy-start(f32[2,256]{1,0:T(2,128)} %param.6) | copy-start | bytes 6148
  16.3 2.4 %copy-start.6 = (f32[22]{0:T(128)S(1)}, f32[22]{0:T(128)}, u32[]{:S(2)}) copy-start(f32[22]{0:T(128)} %add_cosine_fusion.w_ref) | copy-start | bytes 268
  16.3 3.1 %copy-start.4 = (f32[2,256]{1,0:T(2,128)S(1)}, f32[2,256]{1,0:T(2,128)}, u32[]{:S(2)}) copy-start(f32[2,256]{1,0:T(2,128)} %shard_map.55) | copy-start | bytes 6148
  17.0 16.5 %copy-start = (bf16[22,44,256]{2,1,0:T(8,128)(2,1)S(1)}, bf16[22,44,256]{2,1,0:T(8,128)(2,1)}, u32[]{:S(2)}) copy-start(bf16[22,44,256]{2,1,0:T(8,128)(2,1)} %x_ref.1) | copy-start | bytes 1486852
  20.0 25.1 %all-to-all-start = ((f32[64,2,256]{2,1,0:T(2,128)}), f32[64,2,256]{2,1,0:T(2,128)S(1)}, u32[]{:S(2)}, u32[]{:S(2)}) async-start(f32[64,2,256]{2,1,0:T(2,128)} %broadcast_in_dim.33), calls=%async_computation | async-start | bytes 262144 | tf_op jit(solution)/shard_map/all_to_all | solution.py:228
  33.5 3.7 %copy-start.5 = (bf16[26,44,256]{2,1,0:T(8,128)(2,1)}, bf16[26,44,256]{2,1,0:T(8,128)(2,1)S(1)}, u32[]{:S(2)}) copy-start(bf16[26,44,256]{2,1,0:T(8,128)(2,1)S(1)} %constant_dynamic-update-slice_fusion.4.own_ref) | copy-start | bytes 1757188
  33.5 11.6 %collective-permute-start.2 = (bf16[26,44,256]{2,1,0:T(8,128)(2,1)S(1)}, bf16[26,44,256]{2,1,0:T(8,128)(2,1)S(1)}, u32[]{:S(2)}, u32[]{:S(2)}) collective-permute-start(bf16[26,44,256]{2,1,0:T(8,128)(2,1)S(1)} %constant_dynamic-update-slice_fusion.4.own_ref), channel_id=1, source_target_pairs={{1,2},{2,1},{3,4},{4,3},{5,6},{6,5},{7,8},{8,7},{9,10},{10,9},{11,... | collective-permute-start | bytes 1757192 | tf_op jit(solution)/shard_map/ppermute | solution.py:277
  35.1 10.1 %collective-permute-start.3 = (bf16[26,44,256]{2,1,0:T(8,128)(2,1)S(1)}, bf16[26,44,256]{2,1,0:T(8,128)(2,1)S(1)}, u32[]{:S(2)}, u32[]{:S(2)}) collective-permute-start(bf16[26,44,256]{2,1,0:T(8,128)(2,1)S(1)} %constant_dynamic-update-slice_fusion.4.own_ref), channel_id=1, source_target_pairs={{0,1},{1,0},{2,3},{3,2},{4,5},{5,4},{6,7},{7,6},{8,9},{9,8},{10,11... | collective-permute-start | bytes 1757192 | tf_op jit(solution)/shard_map/ppermute | solution.py:272
  45.2 0.7 copy-start.2
  45.2 0.9 copy-start.8
  45.2 1.1 %copy-start.9 = (bf16[26,44,256]{2,1,0:T(8,128)(2,1)}, bf16[26,44,256]{2,1,0:T(8,128)(2,1)S(1)}, u32[]{:S(2)}) copy-start(bf16[26,44,256]{2,1,0:T(8,128)(2,1)S(1)} %collective-permute-done.3.left_right_core) | copy-start | bytes 1757188
  60.7 3.2 %collective-permute-start.5 = (f32[2,256]{1,0:T(2,128)}, f32[2,256]{1,0:T(2,128)S(1)}, u32[]{:S(2)}, u32[]{:S(2)}) collective-permute-start(f32[2,256]{1,0:T(2,128)} %get-tuple-element.8), channel_id=1, source_target_pairs={{0,1},{1,0},{2,3},{3,2},{4,5},{5,4},{6,7},{7,6},{8,9},{9,8},{10,11... | collective-permute-start | bytes 6152 | tf_op jit(solution)/shard_map/ppermute | solution.py:225
  65.3 21.9 %all-to-all-start.1 = ((f32[64,2,256]{2,1,0:T(2,128)}), f32[64,2,256]{2,1,0:T(2,128)S(1)}, u32[]{:S(2)}, u32[]{:S(2)}) async-start(f32[64,2,256]{2,1,0:T(2,128)} %broadcast_in_dim.34), calls=%async_computation.1 | async-start | bytes 262144 | tf_op jit(solution)/shard_map/all_to_all | solution.py:228
  87.2 0.6 copy-start.3

commit v2 on v0

v2 whole, which is shorter than its diff:
```python
import functools
import math

import jax
import jax.numpy as jnp
import numpy as np
from jax import lax
from jax.experimental import pallas as pl
from jax.experimental.pallas import tpu as pltpu
from jax.sharding import Mesh, PartitionSpec as P

BLOCKS = 2
HMAX = 22
TAPS = 2 * HMAX + 1
TILE = 16
SPAN = 64
ROWS = 22
COLS = 44
CHANS = 256
BASIS = 9
N_LAT = 176
N_LON = 704
WIDE = 96
DEEP = BASIS * CHANS
HIGH = BASIS * TILE
LAT = ("y", "xh")
LON = ("z", "core")
F32 = jnp.float32
BF16 = jnp.bfloat16
VMEM_LIMIT = 24 * 1024 * 1024
WEIGHTS = np.cos(np.pi * (np.arange(N_LAT) + 0.5) / N_LAT - np.pi / 2)
TOTAL = float(N_LON * WEIGHTS.sum())


def lat_index():
    return lax.axis_index("y") * 2 + lax.axis_index("xh")


def area_weights(weight_ref):
    row = lax.broadcasted_iota(jnp.int32, (24, CHANS), 0)
    angle = ((lat_index() * ROWS + row).astype(F32) + 0.5) * (math.pi / N_LAT)
    weight = jnp.where(row < ROWS, jnp.sin(angle), 0.0)
    weight_ref[...] = weight
    return COLS * jnp.sum(weight, axis=0, keepdims=True)


def start_all(pairs, sems):
    copies = [pltpu.make_async_copy(s, t, sems.at[n]) for n, (s, t) in enumerate(pairs)]
    for copy in copies:
        copy.start()
    return copies


def put_band(rows, odd, store):
    halves = [None, None]
    for r in range(3):
        place = r + odd
        moved = pltpu.roll(rows[r], SPAN * (place % 2), 1, stride=1, stride_axis=0)
        half = place // 2
        halves[half] = moved if halves[half] is None else halves[half] + moved
    store(slice(0, 128), halves[0].astype(BF16))
    store(slice(128, 256), halves[1].astype(BF16))


def spread(line):
    return jnp.broadcast_to(line, (TILE, 128))


def taps_of(reach_ref, psi_ref, block, i, k):
    tap = lax.broadcasted_iota(jnp.int32, (1, 128), 1) - HMAX
    near = jnp.abs(tap) <= reach_ref[i]
    row = lat_index() * ROWS + i - 1
    taps = []
    for r in range(3):
        keep = near & (row + r >= 0) & (row + r < N_LAT)
        line = jnp.where(keep, psi_ref[k, i, r].astype(F32)[block : block + 1], 0.0)
        taps.append(jnp.broadcast_to(line, (TILE, 128)))
    return taps


def make_bands(reach_ref, psi_ref, block, band_ref, tap_sum_ref, line_ref, sends=()):
    def two_rows(p, _):
        for n in range(2):
            i = 2 * p + n
            for k in range(BASIS):

                def store(lanes, value):
                    band_ref[i, k * TILE : (k + 1) * TILE, lanes] = value

                rows = taps_of(reach_ref, psi_ref, block, i, k)
                put_band(rows, (n + 1 - block) % 2, store)
                line_ref[k, pl.ds(i, 1)] = (rows[0] + rows[1] + rows[2])[0:1]
        return 0

    if sends:
        lax.fori_loop(0, 6, two_rows, 0)
        sends[0].start()
        lax.fori_loop(6, ROWS // 2, two_rows, 0)
        sends[1].start()
    else:
        lax.fori_loop(0, ROWS // 2, two_rows, 0)
    for k in range(BASIS):
        whole = jnp.sum(line_ref[k], axis=1, keepdims=True)
        tap_sum_ref[:, k * CHANS : (k + 1) * CHANS] = jnp.broadcast_to(whole, (ROWS, CHANS))


def prep_kernel(
    reach_ref, x_any, psi_any, sums_ref, mean_ref, edge_ref, band_any, tap_sum_any,
    x_ref, psi_ref, band_ref, tap_sum_ref, line_ref, weight_ref, sems,
):
    x_in, psi_in = start_all([(x_any, x_ref), (psi_any, psi_ref)], sems)
    whole = area_weights(weight_ref)
    x_in.wait()

    def add_row(i, carry):
        first, second = carry
        v = x_ref[i].astype(F32)
        wv = weight_ref[pl.ds(i, 1)] * v
        return first + wv, second + wv * v

    zero = jnp.zeros((COLS, CHANS), F32)
    first, second = lax.fori_loop(0, ROWS, add_row, (zero, zero))
    first = jnp.sum(first, axis=0, keepdims=True)
    sums_ref[0:1] = first
    sums_ref[1:2] = jnp.sum(second, axis=0, keepdims=True)
    mean_ref[...] = first / whole
    psi_in.wait()
    for n in range(2):
        for k in range(BASIS):
            taps = taps_of(reach_ref, psi_ref, 0, n * (ROWS - 1), k)
            for r in range(3):
                edge_ref[n, 3 * k + r : 3 * k + r + 1] = taps[r][0:1]
    half = ROWS // 2
    parts = [(band_ref.at[pl.ds(n * half, half)], band_any.at[pl.ds(n * half, half)]) for n in range(2)]
    sends = [pltpu.make_async_copy(*part, sems.at[2 + n]) for n, part in enumerate(parts)]
    make_bands(reach_ref, psi_ref, 0, band_ref, tap_sum_ref, line_ref, sends)
    sends.append(pltpu.make_async_copy(tap_sum_ref, tap_sum_any, sems.at[4]))
    sends[-1].start()
    for send in sends:
        send.wait()


def message_kernel(
    z_ref, own_any, core_ref, edge_ref, sums_ref, other_ref, a_ref, b_ref, both_ref, sems
):
    xh = lax.axis_index("xh")
    pairs = []
    for n, out in enumerate((a_ref, b_ref)):
        start = jnp.where(xh == n, ROWS - 2, 0)
        pairs.append((own_any.at[pl.ds(start, 2)], out.at[pl.ds(2, 2)]))
    copies = start_all(pairs, sems)
    for n, out in enumerate((a_ref, b_ref)):
        taps = jnp.where(xh == n, edge_ref[1], edge_ref[0])
        start = jnp.where(xh == n, ROWS - 2, 0)
        out[0:2] = z_ref[pl.ds(start, 2)]
        out[4:6] = core_ref[pl.ds(start, 2)]
        out[6] = jnp.zeros((COLS, CHANS), BF16)
        out[6, 0:32, 0:128] = jnp.concatenate([taps, jnp.zeros((5, 128), F32)], axis=0).astype(BF16)
    both_ref[...] = jnp.broadcast_to((sums_ref[...] + other_ref[...])[None], both_ref.shape)
    for copy in copies:
        copy.wait()


def add_kernel(sums_ref, other_ref, both_ref):
    both_ref[...] = jnp.broadcast_to((sums_ref[...] + other_ref[...])[None], both_ref.shape)


def convolve(p, band, u_ref, s_ref, tiles):
    for t in range(tiles):
        window = u_ref[pl.ds(2 * p, 4), TILE * t : TILE * t + SPAN, :].reshape(4 * SPAN, CHANS)
        s = jnp.dot(band, window, preferred_element_type=F32).astype(BF16)
        for ri in range(2):
            for k in range(BASIS):
                at = (ri * BASIS + k) * TILE
                s_ref[2 * p + ri, TILE * t : TILE * t + TILE, k * CHANS : (k + 1) * CHANS] = s[
                    at : at + TILE
                ]


def first_conv_kernel(
    mean_ref, z_ref, core_ref, a_ref, b_ref, own_any, band_any, s_any, tap_sum_any, res_any,
    tap_sum_ref, res_ref, u_ref, edge_ref, own_ref, band_ref, s_ref, in_sems, out_sems,
):
    own_in, band_in = start_all([(own_any, own_ref), (band_any, band_ref)], in_sems)
    xh, core = lax.axis_index("xh"), lax.axis_index("core")
    local_mean = mean_ref[...]

    def put_row(r, from_z, own, from_core):
        from_z, own, from_core = from_z.astype(F32), own.astype(F32), from_core.astype(F32)
        left = jnp.where(core == 0, from_z, from_core)
        right = jnp.where(core == 0, from_core, from_z)
        pad = jnp.zeros((12, CHANS), F32)
        u_ref[r] = (jnp.concatenate([left, own, right, pad], axis=0) - local_mean).astype(BF16)
        res = jnp.concatenate([left[HMAX:], own, right[:HMAX], pad[:8]], axis=0)
        return res.astype(BF16)

    def own_row(i, _):
        res_ref[i + 1] = put_row(i + 2, z_ref[i], own_ref[i], core_ref[i])
        return 0

    own_in.wait()
    lax.fori_loop(0, ROWS, own_row, 0)
    band_in.wait()

    def rim(piece, upper):
        use_b = (xh == 0) if upper else (xh == 1)
        return jnp.where(use_b, b_ref[piece].astype(F32), a_ref[piece].astype(F32))

    for upper in (True, False):
        for j in range(2):
            res = put_row(
                j if upper else ROWS + 2 + j, rim(j, upper), rim(2 + j, upper), rim(4 + j, upper)
            )
            if j == (1 if upper else 0):
                res_ref[0 if upper else ROWS + 1] = res
        place = 0 if upper else 1
        lines = rim(6, upper)[:, :128]
        for k in range(BASIS):

            def store(lanes, value):
                edge_ref[place, k * TILE : (k + 1) * TILE, lanes] = value

            rows = [spread(lines[3 * k + r : 3 * k + r + 1]) for r in range(3)]
            put_band(rows, place, store)
            whole = jnp.sum((rows[0] + rows[1] + rows[2])[0:1], axis=1, keepdims=True)
            tap_sum_ref[place : place + 1, k * CHANS : (k + 1) * CHANS] = jnp.broadcast_to(
                whole, (1, CHANS)
            )

    tiles = WIDE // TILE
    rest = [
        pltpu.make_async_copy(tap_sum_ref, tap_sum_any, in_sems.at[2]),
        pltpu.make_async_copy(res_ref, res_any, in_sems.at[3]),
    ]
    for send_rest in rest:
        send_rest.start()

    def send(p):
        at = pl.ds(2 * p, 2)
        return pltpu.make_async_copy(s_ref.at[at], s_any.at[at], out_sems.at[p])

    def one_pair(p, _):
        band = band_ref[pl.ds(2 * p - 1, 2)].reshape(2 * HIGH, 4 * SPAN)
        convolve(p, band, u_ref, s_ref, tiles)
        send(p).start()
        return 0

    convolve(0, jnp.concatenate([edge_ref[0], band_ref[0]], axis=0), u_ref, s_ref, tiles)
    send(0).start()
    lax.fori_loop(1, ROWS // 2, one_pair, 0)
    convolve(ROWS // 2, jnp.concatenate([band_ref[ROWS - 1], edge_ref[1]], axis=0), u_ref, s_ref, tiles)
    send(ROWS // 2).start()

    def end(p, _):
        send(p).wait()
        return 0

    lax.fori_loop(0, ROWS // 2 + 1, end, 0)
    for send_rest in rest:
        send_rest.wait()


def scale_of(gathered_ref, gain):
    total = jnp.sum(gathered_ref[...], axis=0)
    mean = total[0:1] / TOTAL
    scale = lax.rsqrt(total[1:2] / TOTAL - mean * mean + 1e-05) * gain
    diagonal = lax.broadcasted_iota(jnp.int32, (CHANS, CHANS), 0) == lax.broadcasted_iota(
        jnp.int32, (CHANS, CHANS), 1
    )
    return mean, jnp.sum(jnp.where(diagonal, scale, 0.0), axis=1, keepdims=True)


def scale_mixing(column, mix_ref, scaled_ref):
    for k in range(BASIS):
        scaled_ref[k * CHANS : (k + 1) * CHANS] = (mix_ref[k].astype(F32) * column).astype(BF16)


def shift_rows(tap_sum, shift, scaled_ref):
    lhs = tap_sum * jnp.concatenate([shift] * BASIS, axis=1)
    high = lhs.astype(BF16)
    low = (lhs - high.astype(F32)).astype(BF16)
    scaled = scaled_ref[...]
    return jnp.dot(high, scaled, preferred_element_type=F32) + jnp.dot(
        low, scaled, preferred_element_type=F32
    )


def first_mix_kernel(
    gathered_ref, local_mean_ref, gain_any, edge_sum_any, mix_any, s_any, tap_sum_any, res_any,
    mid_any, scaled_any, shift_any, sums_ref, new_mean_ref,
    gain_ref, edge_sum_ref, shift_ref, mix_ref, s_ref, tap_sum_ref, res_ref, mid_ref, scaled_ref, weight_ref, in_sems, out_sems,
):
    mid = 4 * TILE
    parts = (6, 8, 8)
    spans = [(sum(parts[:g]), parts[g]) for g in range(len(parts))]
    of_mid = pl.ds(TILE, mid)
    pairs = [
        (mix_any.at[0], mix_ref),
        (tap_sum_any, tap_sum_ref),
        (res_any.at[pl.ds(1, ROWS), of_mid], res_ref),
        (gain_any, gain_ref),
        (edge_sum_any, edge_sum_ref),
    ] + [(s_any.at[pl.ds(at + 1, n), of_mid], s_ref.at[pl.ds(at, n)]) for at, n in spans]
    mix_in, tap_in, res_in, gain_in, edge_in, *s_in = [
        pltpu.make_async_copy(s, t, in_sems.at[n]) for n, (s, t) in enumerate(pairs)
    ]
    for now in (gain_in, mix_in, tap_in, edge_in, s_in[0]):
        now.start()
    whole = area_weights(weight_ref)
    gain_in.wait()
    mean, column = scale_of(gathered_ref, gain_ref[0:1])
    shift = local_mean_ref[...] - mean
    mix_in.wait()
    for later in (s_in[1], res_in, s_in[2]):
        later.start()
    scale_mixing(column, mix_ref, scaled_ref)
    send_scaled = pltpu.make_async_copy(scaled_ref, scaled_any, out_sems.at[0])
    send_scaled.start()
    tap_in.wait()
    edge_in.wait()
    shift_ref[0:ROWS] = shift_rows(tap_sum_ref[...], shift, scaled_ref)
    shift_ref[ROWS : ROWS + 2] = shift_rows(edge_sum_ref[...], shift, scaled_ref)
    column = lax.broadcasted_iota(jnp.int32, (mid, CHANS), 0) + TILE
    mine = (column >= HMAX) & (column < HMAX + COLS)
    first = second = jnp.zeros((mid, CHANS), F32)
    send_shift = pltpu.make_async_copy(shift_ref, shift_any, out_sems.at[4])
    send_shift.start()
    sends = [send_scaled, send_shift]
    for g, (at, n) in enumerate(spans):
        s_in[g].wait()
        lhs = s_ref[at : at + n].reshape(n * mid, DEEP)
        conv = jnp.dot(lhs, scaled_ref[...], preferred_element_type=F32).reshape(n, mid, CHANS)
        if g == 0:
            res_in.wait()
        for i in range(at, at + n):
            grown = jax.nn.gelu(conv[i - at] + shift_ref[i : i + 1])
            new = (res_ref[i].astype(F32) + grown).astype(BF16)
            mid_ref[i] = new
            v = jnp.where(mine, new.astype(F32), 0.0)
            wv = weight_ref[i : i + 1] * v
            first, second = first + wv, second + wv * v
        span = pl.ds(at, n)
        sends.append(pltpu.make_async_copy(mid_ref.at[span], mid_any.at[span], out_sems.at[1 + g]))
        sends[-1].start()
    first = jnp.sum(first, axis=0, keepdims=True)
    sums_ref[0:1] = first
    sums_ref[1:2] = jnp.sum(second, axis=0, keepdims=True)
    new_mean_ref[...] = first / whole
    for send in sends:
        send.wait()


def second_conv_kernel(
    reach_ref, mean_ref, shift_any, psi_any, scaled_any, res_any, mid_any, s_any, tap_sum_any, out_any,
    tap_sum_ref, shift_ref, u_ref, s_ref, rows_ref, out_ref, psi_ref, scaled_ref, res_ref, mid_ref, band_ref, line_ref,
    in_sems, out_sems,
):
    psi_in, *fetches, mid_in = start_all(
        [(psi_any, psi_ref), (scaled_any, scaled_ref), (res_any, res_ref)]
        + [
            (s_any.at[pl.ds(1, ROWS), pl.ds(n * (WIDE - TILE), TILE)], s_ref.at[n])
            for n in range(2)
        ]
        + [(s_any.at[n * (ROWS + 1)], rows_ref.at[n]) for n in range(2)]
        + [(shift_any, shift_ref), (mid_any, mid_ref)],
        in_sems,
    )
    local_mean = mean_ref[...]
    psi_in.wait()
    make_bands(reach_ref, psi_ref, 1, band_ref, tap_sum_ref, line_ref)
    tap_out = pltpu.make_async_copy(tap_sum_ref, tap_sum_any, in_sems.at[10])
    tap_out.start()

    for fetch in fetches:
        fetch.wait()
    for left in range(2):
        at = slice(left * (WIDE - TILE), left * (WIDE - TILE) + TILE)
        lhs = s_ref[left].reshape(ROWS * TILE, DEEP)
        conv = jnp.dot(lhs, scaled_ref[...], preferred_element_type=F32).reshape(ROWS, TILE, CHANS)
        for i in range(ROWS):
            grown = jax.nn.gelu(conv[i] + shift_ref[i : i + 1])
            new = (res_ref[i + 1, at].astype(F32) + grown).astype(BF16).astype(F32)
            u_ref[i + 1, at] = (new - local_mean).astype(BF16)
    lhs = rows_ref[...].reshape(2 * WIDE, DEEP)
    conv = jnp.dot(lhs, scaled_ref[...], preferred_element_type=F32).reshape(2, WIDE, CHANS)
    for n in range(2):
        e = n * (ROWS + 1)
        grown = jax.nn.gelu(conv[n] + shift_ref[ROWS + n : ROWS + n + 1])
        new = (res_ref[e].astype(F32) + grown).astype(BF16).astype(F32)
        u_ref[e] = (new - local_mean).astype(BF16)

    mid_in.wait()

    def mid_row(i, _):
        u_ref[i + 1, TILE : 5 * TILE] = (mid_ref[i].astype(F32) - local_mean).astype(BF16)
        return 0

    lax.fori_loop(0, ROWS, mid_row, 0)

    def one_pair(p, _):
        band = band_ref[pl.ds(2 * p, 2)].reshape(2 * HIGH, 4 * SPAN)
        convolve(p, band, u_ref, out_ref, 3)
        send(p).start()
        return 0

    def send(p):
        at = pl.ds(2 * p, 2)
        return pltpu.make_async_copy(out_ref.at[at], out_any.at[at], out_sems.at[p])

    def end(p, _):
        send(p).wait()
        return 0

    lax.fori_loop(0, ROWS // 2, one_pair, 0)
    lax.fori_loop(0, ROWS // 2, end, 0)
    tap_out.wait()


def second_mix_kernel(
    gathered_ref, local_mean_ref, gain_any, mix_any, s_any, tap_sum_any, mid_any, out_any,
    gain_ref, mix_ref, s_ref, tap_sum_ref, mid_ref, scaled_ref, shift_ref, out_ref, in_sems, out_sems,
):
    cols = 3 * TILE
    parts = (6, 8, 8)
    spans = [(sum(parts[:g]), parts[g]) for g in range(len(parts))]
    pairs = [
        (mix_any.at[1], mix_ref),
        (tap_sum_any, tap_sum_ref),
        (mid_any, mid_ref),
        (gain_any, gain_ref),
    ] + [
        (s_any.at[pl.ds(at, n)], s_ref.at[pl.ds(at, n)]) for at, n in spans
    ]
    mix_in, tap_in, mid_in, gain_in, *s_in = [
        pltpu.make_async_copy(s, t, in_sems.at[n]) for n, (s, t) in enumerate(pairs)
    ]
    for now in (gain_in, mix_in, tap_in, s_in[0]):
        now.start()
    gain_in.wait()
    mean, column = scale_of(gathered_ref, gain_ref[1:2])
    shift = local_mean_ref[...] - mean
    mix_in.wait()
    for later in (s_in[1], mid_in, s_in[2]):
        later.start()
    scale_mixing(column, mix_ref, scaled_ref)
    tap_in.wait()
    shift_ref[...] = shift_rows(tap_sum_ref[...], shift, scaled_ref)
    sends = []
    for g, (at, n) in enumerate(spans):
        s_in[g].wait()
        lhs = s_ref[at : at + n].reshape(n * cols, DEEP)
        conv = jnp.dot(lhs, scaled_ref[...], preferred_element_type=F32).reshape(n, cols, CHANS)
        if g == 0:
            mid_in.wait()
        for i in range(at, at + n):
            grown = jax.nn.gelu(conv[i - at] + shift_ref[i : i + 1])
            res = mid_ref[i].astype(F32)[HMAX - TILE : HMAX - TILE + COLS]
            out_ref[i] = (res + grown[:COLS]).astype(BF16)
        span = pl.ds(at, n)
        sends.append(pltpu.make_async_copy(out_ref.at[span], out_any.at[span], out_sems.at[g]))
        sends[-1].start()
    for send in sends:
        send.wait()


def shape(*dims, dtype=BF16):
    return jax.ShapeDtypeStruct(dims, dtype)


SMEM = pl.BlockSpec(memory_space=pltpu.SMEM)
VMEM = pl.BlockSpec(memory_space=pltpu.VMEM)
HBM = pl.BlockSpec(memory_space=pltpu.HBM)


def call(kernel, ins, outs, scratch=(), flops=10**6):
    run = pl.pallas_call(
        kernel,
        out_shape=[pltpu.HBM(o.shape, o.dtype) if spec is HBM else o for o, spec in outs],
        in_specs=ins,
        out_specs=[spec for _, spec in outs],
        scratch_shapes=list(scratch),
        compiler_params=pltpu.CompilerParams(vmem_limit_bytes=VMEM_LIMIT),
        cost_estimate=pl.CostEstimate(flops=flops, bytes_accessed=10**6, transcendentals=0),
    )

    def placed(*values):
        return run(
            *[
                pltpu.with_memory_space_constraint(v, pltpu.HBM) if spec is HBM else v
                for v, spec in zip(values, ins)
            ]
        )

    return placed


def swap_pairs(count, first):
    pairs = []
    for i in range(first, count - 1, 2):
        pairs += [(i, i + 1), (i + 1, i)]
    return pairs


def from_other_core(v):
    return lax.ppermute(v, "core", [(0, 1), (1, 0)])


def gather(both):
    return lax.all_to_all(both, ("y", "xh", "z"), 0, 0)


def buffer(*dims):
    return pltpu.VMEM(dims, BF16)


def semaphores(count):
    return pltpu.SemaphoreType.DMA((count,))


def floats(*dims):
    return pltpu.VMEM(dims, F32)


def local(x, norm_gain, mixing, kernel_psi, lon_reach):
    peers = lax.axis_size("y") * lax.axis_size("xh") * lax.axis_size("z")
    sums_out = (shape(2, CHANS, dtype=F32), VMEM)
    mean_out = (shape(1, CHANS, dtype=F32), VMEM)
    both_out = (shape(peers, 2, CHANS, dtype=F32), VMEM)
    tap_sum_out = (shape(ROWS, DEEP, dtype=F32), HBM)
    mid_cols, own_cols = 4 * TILE, 3 * TILE

    from_core = from_other_core(x)
    ring = []
    for z in range(8):
        a, b = 2 * z + 1, (2 * z + 2) % 16
        ring += [(a, b), (b, a)]
    from_z = lax.ppermute(x, LON, ring)

    psi = jnp.transpose(kernel_psi, (1, 2, 3, 0, 4))
    psi = jnp.pad(psi, ((0, 0),) * 4 + ((0, 128 - TAPS),))
    sums, mean, edge, band1, tap_sum1 = call(
        prep_kernel,
        [SMEM, HBM, HBM],
        [
            sums_out,
            mean_out,
            (shape(2, 3 * BASIS, 128, dtype=F32), VMEM),
            (shape(ROWS, HIGH, 4 * SPAN), HBM),
            tap_sum_out,
        ],
        [
            buffer(ROWS, COLS, CHANS),
            buffer(BASIS, ROWS, 3, BLOCKS, 128),
            buffer(ROWS, HIGH, 4 * SPAN),
            floats(ROWS, DEEP),
            floats(BASIS, ROWS, 128),
            floats(24, CHANS),
            semaphores(5),
        ],
    )(lon_reach, x, psi)

    message = (shape(7, COLS, CHANS), VMEM)
    to_a, to_b, both = call(
        message_kernel, [VMEM, HBM] + [VMEM] * 4, [message, message, both_out], [semaphores(2)]
    )(from_z, x, from_core, edge, sums, from_other_core(sums))
    got_a = lax.ppermute(to_a, LAT, swap_pairs(8, 0))
    got_b = lax.ppermute(to_b, LAT, swap_pairs(8, 1))
    gathered = gather(both)

    s1, edge_sum, res = call(
        first_conv_kernel,
        [VMEM] * 5 + [HBM] * 2,
        [
            (shape(ROWS + 2, WIDE, DEEP), HBM),
            (shape(2, DEEP, dtype=F32), HBM),
            (shape(ROWS + 2, WIDE, CHANS), HBM),
        ],
        [
            floats(2, DEEP),
            buffer(ROWS + 2, WIDE, CHANS),
            buffer(ROWS + 4, 144, CHANS),
            buffer(2, HIGH, 4 * SPAN),
            buffer(ROWS, COLS, CHANS),
            buffer(ROWS, HIGH, 4 * SPAN),
            buffer(ROWS + 2, WIDE, DEEP),
            semaphores(4),
            semaphores(12),
        ],
        flops=4 * 10**9,
    )(mean, from_z, from_core, got_a, got_b, x, band1)
    mid, scaled, shift, sums1, mean1 = call(
        first_mix_kernel,
        [VMEM] * 2 + [HBM] * 6,
        [
            (shape(ROWS, mid_cols, CHANS), HBM),
            (shape(DEEP, CHANS), HBM),
            (shape(ROWS + 2, CHANS, dtype=F32), HBM),
            sums_out,
            mean_out,
        ],
        [
            floats(BLOCKS, CHANS),
            floats(2, DEEP),
            floats(ROWS + 2, CHANS),
            buffer(BASIS, CHANS, CHANS),
            buffer(ROWS, mid_cols, DEEP),
            floats(ROWS, DEEP),
            buffer(ROWS, mid_cols, CHANS),
            buffer(ROWS, mid_cols, CHANS),
            buffer(DEEP, CHANS),
            floats(24, CHANS),
            semaphores(8),
            semaphores(5),
        ],
        flops=2 * 10**9,
    )(gathered, mean, norm_gain, edge_sum, mixing, s1, tap_sum1, res)
    (both1,) = call(add_kernel, [VMEM, VMEM], [both_out])(sums1, from_other_core(sums1))
    gathered1 = gather(both1)
    tap_sum2, s2 = call(
        second_conv_kernel,
        [SMEM, VMEM] + [HBM] * 6,
        [tap_sum_out, (shape(ROWS, own_cols, DEEP), HBM)],
        [
            floats(ROWS, DEEP),
            floats(ROWS + 2, CHANS),
            buffer(ROWS + 2, WIDE, CHANS),
            buffer(2, ROWS, TILE, DEEP),
            buffer(2, WIDE, DEEP),
            buffer(ROWS, own_cols, DEEP),
            buffer(BASIS, ROWS, 3, BLOCKS, 128),
            buffer(DEEP, CHANS),
            buffer(ROWS + 2, WIDE, CHANS),
            buffer(ROWS, mid_cols, CHANS),
            buffer(ROWS, HIGH, 4 * SPAN),
            floats(BASIS, ROWS, 128),
            semaphores(11),
            semaphores(11),
        ],
        flops=3 * 10**9,
    )(lon_reach, mean1, shift, psi, scaled, res, mid, s1)
    (out,) = call(
        second_mix_kernel,
        [VMEM] * 2 + [HBM] * 5,
        [(shape(ROWS, COLS, CHANS), HBM)],
        [
            floats(BLOCKS, CHANS),
            buffer(BASIS, CHANS, CHANS),
            buffer(ROWS, own_cols, DEEP),
            floats(ROWS, DEEP),
            buffer(ROWS, mid_cols, CHANS),
            buffer(DEEP, CHANS),
            floats(ROWS, CHANS),
            buffer(ROWS, COLS, CHANS),
            semaphores(7),
            semaphores(3),
        ],
        flops=2 * 10**9,
    )(gathered1, mean1, norm_gain, mixing, s2, tap_sum2, mid)
    return out


def solution(mesh):
    split = Mesh(mesh.devices.reshape(2, 4, 2, 8, 2), ("mem", "y", "xh", "z", "core"))
    placed = (P(LAT, LON, "mem"), P(), P(), P(None, None, LAT, None, None), P(LAT))
    return jax.shard_map(
        local, mesh=split, in_specs=placed, out_specs=P(LAT, LON, "mem"), check_vma=False
    )
```

time: 1160 us -> 82 us (0.07)
  blocking collectives: 653 us -> 0 us
  local copies, waits for them, and re-layouts: 342 us -> 2.66 us
  other arithmetic: 68.5 us -> 0 us
  matrix products: 64.4 us -> 0 us
  Pallas kernels: 0 us -> 37.9 us
    psum x2 -> x0, blocking collectives: 653 us -> none  [local(): lax.psum((jnp.sum(weighted * values, axis=(0, 1)), jnp.sum(weighted * val...]
    gather x2 -> x0, local copies, waits for them, and re-layouts: 209 us -> none  [band_matrix(): taken = jnp.take(psi_block, tap_place, axis=3)]
    reshape x2 -> x0, local copies, waits for them, and re-layouts: 90.3 us -> none  [band_matrix(): taken.reshape(psi_block.shape[0], psi_block.shape[1], 3, columns, width)]
    dot_general x72 -> x0, matrix products: 64.4 us -> none  [the longest x54 34.2 us: contract(): jnp.einsum('iab,ibc->iac', band_basis[:, shift], basis_field[shift:shift...]
    select_n x3 -> x0, other arithmetic: 57.7 us -> none  [the longest x2 46.2 us: band_matrix(): taken = jnp.take(psi_block, tap_place, axis=3)]
    pallas_call x0 -> x7, Pallas kernels: none -> 37.9 us  [placed(): run(*[pltpu.with_memory_space_constraint(v, pltpu.HBM) if spec is HBM els...]
    squeeze x22 -> x0, local copies, waits for them, and re-layouts: 25.3 us -> none  [the longest x18 23.2 us: add_input(): band_basis = lax.dynamic_index_in_dim(band_mats, basis, 0, keepdims=False)]
    all_to_all x0 -> x2, starting transfers between devices: none -> 19.2 us  [gather(): return lax.all_to_all(both, ('y', 'xh', 'z'), 0, 0)]
  transfers between devices with their start and end apart: 8 -> 8, of which waited for: 2 -> 4; matrix products, arithmetic and copies ran while one was open for 31% -> 2% of each run, Pallas kernels for 0% -> 27%
where the time goes in v2:
time: 82 us; the launch traced here: 81.6 us
  Pallas kernels  37.9 us (46%)
  starting transfers between devices  33.2 us (40%)
  waiting for transfers between devices  7.62 us (9%)
  local copies, waits for them, and re-layouts  2.66 us (3%)
    pallas_call x7, Pallas kernels, placed(): run(*[pltpu.with_memory_space_constraint(v, pltpu.HBM) if spec is HBM els...  37.9 us
    all_to_all x2, starting transfers between devices, gather(): return lax.all_to_all(both, ('y', 'xh', 'z'), 0, 0)  19.2 us
    ppermute x3, starting transfers between devices, from_other_core(): return lax.ppermute(v, 'core', [(0, 1), (1, 0)])  10.5 us
    all_to_all x2, waiting for transfers between devices, gather(): return lax.all_to_all(both, ('y', 'xh', 'z'), 0, 0)  5.97 us
    ppermute x1, starting transfers between devices, local(): got_a = lax.ppermute(to_a, LAT, swap_pairs(8, 0))  2.83 us
    pad x1, local copies, waits for them, and re-layouts, local(): psi = jnp.pad(psi, ((0, 0),) * 4 + ((0, 128 - TAPS),))  2 us
    ppermute x3, waiting for transfers between devices, from_other_core(): return lax.ppermute(v, 'core', [(0, 1), (1, 0)])  1.64 us
  transfers between devices with their start and end apart: 8, of which 4 were waited for; matrix products, arithmetic and copies ran while one was open for 2% of the time, Pallas kernels for 27%

profile of v2, /device:TPU:1, one launch (start us, length us, event | category | flops | bytes accessed | tf_op | source)
XLA Modules:
  0.0 81.6 jit_solution(11291302629655164358)
XLA Ops:
  0.0 3.2 %collective-permute-start.1 = (bf16[22,44,256]{2,1,0:T(8,128)(2,1)}, bf16[22,44,256]{2,1,0:T(8,128)(2,1)S(1)}, u32[]{:S(2)}, u32[]{:S(2)}) collective-permute-start(bf16[22,44,256]{2,1,0:T(8,128)(2,1)} %own_any.3), channel_id=1, source_target_pairs={{0,1},{1,0},{2,3},{3,2},{4,5},{5,4},{6,7},{7,6},{8,9},{9,8},{10,11... | collective-permute-start | bytes 1486856 | tf_op jit(solution)/shard_map/ppermute | solution.py:505
  3.2 0.0 collective-permute-start
  3.2 2.0 %pad.4.psi_any = bf16[9,22,3,2,128]{4,3,2,1,0:T(2,128)(2,1)} pad(bf16[9,22,3,2,45]{4,3,2,1,0:T(2,128)(2,1)} %bitcast.1, bf16[]{:T(256)} %constant.2.clone.1), padding=0_0x0_0x0_0x0_0x0_83 | pad | bytes 411050 | tf_op jit(solution)/shard_map/jit(_pad)/pad | solution.py:540
  5.2 0.7 copy-done
  5.9 4.9 %shard_map.55 = (f32[2,256]{1,0:T(2,128)S(1)}, f32[1,256]{1,0:T(1,128)S(1)}, f32[2,27,128]{2,1,0:T(8,128)S(1)}, bf16[22,144,256]{2,1,0:T(8,128)(2,1)}, f32[22,2304]{1,0:T(8,128)}) custom-call(s32[22]{0:T(128)S(1)} %copy-done, bf16[22,44,256]{2,1,0:T(8,128)(2,1)} %own_any.3, bf16[9,22,3,2,128]{4,3,2,1,0:T(2,128)(2,1)} %pad.4.psi_any), custom_call_target="tpu_custom_call" | custom-call | flops 1000000 | bytes 1000000 | tf_op jit(solution)/shard_map/pallas_call | solution.py:487
  10.8 4.3 %collective-permute-start.2 = (f32[2,256]{1,0:T(2,128)S(1)}, f32[2,256]{1,0:T(2,128)S(1)}, u32[]{:S(2)}, u32[]{:S(2)}) collective-permute-start(f32[2,256]{1,0:T(2,128)S(1)} %get-tuple-element.24.sums_ref), channel_id=1, source_target_pairs={{0,1},{1,0},{2,3},{3,2},{4,5},{5,4},{6,7},{7,6},{8,9},{9,8},{10,11... | collective-permute-start | bytes 6152 | tf_op jit(solution)/shard_map/ppermute | solution.py:505
  15.1 0.8 %collective-permute-done.2.other_ref = f32[2,256]{1,0:T(2,128)S(1)} collective-permute-done((f32[2,256]{1,0:T(2,128)S(1)}, f32[2,256]{1,0:T(2,128)S(1)}, u32[]{:S(2)}, u32[]{:S(2)}) %collective-permute-start.2) | collective-permute-done | bytes 2080 | tf_op jit(solution)/shard_map/ppermute | solution.py:505
  15.9 0.0 collective-permute-done.1.core_ref
  15.9 0.0 collective-permute-done.z_ref
  15.9 1.5 %shard_map.56 = (bf16[7,44,256]{2,1,0:T(8,128)(2,1)S(1)}, bf16[7,44,256]{2,1,0:T(8,128)(2,1)S(1)}, f32[64,2,256]{2,1,0:T(2,128)}) custom-call(bf16[22,44,256]{2,1,0:T(8,128)(2,1)S(1)} %collective-permute-done.z_ref, bf16[22,44,256]{2,1,0:T(8,128)(2,1)} %own_any.3, bf16[22,44,256]{2,1,0:T(8,128)(2,1)S(1)} %collective-permute-done.1.core_ref, ...), custom_call_target="tpu_custom_call" | custom-call | flops 1000000 | bytes 1000000 | tf_op jit(solution)/shard_map/pallas_call | solution.py:487
  17.4 2.8 %collective-permute-start.3 = (bf16[7,44,256]{2,1,0:T(8,128)(2,1)S(1)}, bf16[7,44,256]{2,1,0:T(8,128)(2,1)S(1)}, u32[]{:S(2)}, u32[]{:S(2)}) collective-permute-start(bf16[7,44,256]{2,1,0:T(8,128)(2,1)S(1)} %get-tuple-element.27), channel_id=1, source_target_pairs={{0,16},{16,0},{32,48},{48,32},{64,80},{80,64},{96,112},{112,96},{1... | collective-permute-start | bytes 473096 | tf_op jit(solution)/shard_map/ppermute | solution.py:566
  20.3 0.7 collective-permute-start.4
  20.9 11.5 %all-to-all-start = ((f32[64,2,256]{2,1,0:T(2,128)}), f32[64,2,256]{2,1,0:T(2,128)S(1)}, u32[]{:S(2)}, u32[]{:S(2)}) async-start(f32[64,2,256]{2,1,0:T(2,128)} %get-tuple-element.25), calls=%async_computation | async-start | bytes 262144 | tf_op jit(solution)/shard_map/all_to_all | solution.py:509
  32.4 0.0 collective-permute-done.3.a_ref
  32.4 7.7 %shard_map.57 = (bf16[24,96,2304]{2,1,0:T(8,128)(2,1)}, f32[2,2304]{1,0:T(2,128)}, bf16[24,96,256]{2,1,0:T(8,128)(2,1)}) custom-call(f32[1,256]{1,0:T(1,128)S(1)} %get-tuple-element.26.mean_ref.local_mean_ref, bf16[22,44,256]{2,1,0:T(8,128)(2,1)S(1)} %collective-permute-done.z_ref, bf16[22,44,256]{2,1,0:T(8,128)(2,1)S(1)} %collective-permute-done.1.core_ref, ...), custom_call_target="tpu_custom_call" | custom-call | flops 4000000000 | bytes 1000000 | tf_op jit(solution)/shard_map/pallas_call | solution.py:487
  40.2 3.7 %all-to-all-done.gathered_ref = f32[64,2,256]{2,1,0:T(2,128)S(1)} async-done(((f32[64,2,256]{2,1,0:T(2,128)}), f32[64,2,256]{2,1,0:T(2,128)S(1)}, u32[]{:S(2)}, u32[]{:S(2)}) %all-to-all-start) | async-done | bytes 131104 | tf_op jit(solution)/shard_map/all_to_all | solution.py:509
  43.9 7.5 %shard_map.58 = (bf16[22,64,256]{2,1,0:T(8,128)(2,1)}, bf16[2304,256]{1,0:T(8,128)(2,1)}, f32[24,256]{1,0:T(8,128)}, f32[2,256]{1,0:T(2,128)S(1)}, f32[1,256]{1,0:T(1,128)S(1)}) custom-call(f32[64,2,256]{2,1,0:T(2,128)S(1)} %all-to-all-done.gathered_ref, f32[1,256]{1,0:T(1,128)S(1)} %get-tuple-element.26.mean_ref.local_mean_ref, f32[2,256]{1,0:T(2,128)} %gain_any.3, ...), custom_call_target="tpu_custom_call" | custom-call | flops 2000000000 | bytes 1000000 | tf_op jit(solution)/shard_map/pallas_call | solution.py:487
  51.4 3.0 %collective-permute-start.5 = (f32[2,256]{1,0:T(2,128)S(1)}, f32[2,256]{1,0:T(2,128)S(1)}, u32[]{:S(2)}, u32[]{:S(2)}) collective-permute-start(f32[2,256]{1,0:T(2,128)S(1)} %get-tuple-element.34.sums_ref), channel_id=1, source_target_pairs={{0,1},{1,0},{2,3},{3,2},{4,5},{5,4},{6,7},{7,6},{8,9},{9,8},{10,11... | collective-permute-start | bytes 6152 | tf_op jit(solution)/shard_map/ppermute | solution.py:505
  54.3 0.8 %collective-permute-done.5.other_ref = f32[2,256]{1,0:T(2,128)S(1)} collective-permute-done((f32[2,256]{1,0:T(2,128)S(1)}, f32[2,256]{1,0:T(2,128)S(1)}, u32[]{:S(2)}, u32[]{:S(2)}) %collective-permute-start.5) | collective-permute-done | bytes 2080 | tf_op jit(solution)/shard_map/ppermute | solution.py:505
  55.2 0.7 shard_map.59
  55.8 7.7 %all-to-all-start.1 = ((f32[64,2,256]{2,1,0:T(2,128)}), f32[64,2,256]{2,1,0:T(2,128)S(1)}, u32[]{:S(2)}, u32[]{:S(2)}) async-start(f32[64,2,256]{2,1,0:T(2,128)} %shard_map.59), calls=%async_computation.1 | async-start | bytes 262144 | tf_op jit(solution)/shard_map/all_to_all | solution.py:509
  63.5 9.4 %shard_map.60 = (f32[22,2304]{1,0:T(8,128)}, bf16[22,48,2304]{2,1,0:T(8,128)(2,1)}) custom-call(s32[22]{0:T(128)S(1)} %copy-done.1, f32[1,256]{1,0:T(1,128)S(1)} %get-tuple-element.35.mean_ref.local_mean_ref, f32[24,256]{1,0:T(8,128)} %get-tuple-element.36.shift_any, bf16[9,22,3,2,128]{4,3,2,1,0:T(2,128)(2,1)} %pad.4.psi_any, ...), custom_call_target="tpu_custom_call" | custom-call | flops 3000000000 | bytes 1000000 | tf_op jit(solution)/shard_map/pallas_call | solution.py:487
  72.9 2.2 %all-to-all-done.1.gathered_ref = f32[64,2,256]{2,1,0:T(2,128)S(1)} async-done(((f32[64,2,256]{2,1,0:T(2,128)}), f32[64,2,256]{2,1,0:T(2,128)S(1)}, u32[]{:S(2)}, u32[]{:S(2)}) %all-to-all-start.1) | async-done | bytes 131104 | tf_op jit(solution)/shard_map/all_to_all | solution.py:509
  75.1 6.3 %shard_map.61 = bf16[22,44,256]{2,1,0:T(8,128)(2,1)} custom-call(f32[64,2,256]{2,1,0:T(2,128)S(1)} %all-to-all-done.1.gathered_ref, f32[1,256]{1,0:T(1,128)S(1)} %get-tuple-element.35.mean_ref.local_mean_ref, f32[2,256]{1,0:T(2,128)} %gain_any.3, bf16[2,9,256,256]{3,2,1,0:T(8,128)(2,1)} %mix_any.3, bf16[22,48,2304]{2,1,0:T(8,128)(2,1)} %get-tuple-element.39.s_any, ...), custom_call_target="tpu_custom_call" | custom-call | flops 2000000000 | bytes 1000000 | tf_op jit(solution)/shard_map/pallas_call | solution.py:487
  (4 shorter events, 0.0 us)
Async XLA Ops:
  0.0 15.9 %collective-permute-start.1 = (bf16[22,44,256]{2,1,0:T(8,128)(2,1)}, bf16[22,44,256]{2,1,0:T(8,128)(2,1)S(1)}, u32[]{:S(2)}, u32[]{:S(2)}) collective-permute-start(bf16[22,44,256]{2,1,0:T(8,128)(2,1)} %own_any.3), channel_id=1, source_target_pairs={{0,1},{1,0},{2,3},{3,2},{4,5},{5,4},{6,7},{7,6},{8,9},{9,8},{10,11... | collective-permute-start | bytes 1486856 | tf_op jit(solution)/shard_map/ppermute | solution.py:505
  3.2 12.7 %collective-permute-start = (bf16[22,44,256]{2,1,0:T(8,128)(2,1)}, bf16[22,44,256]{2,1,0:T(8,128)(2,1)S(1)}, u32[]{:S(2)}, u32[]{:S(2)}) collective-permute-start(bf16[22,44,256]{2,1,0:T(8,128)(2,1)} %own_any.3), channel_id=1, source_target_pairs={{1,2},{2,1},{3,4},{4,3},{5,6},{6,5},{7,8},{8,7},{9,10},{10,9},{11,... | collective-permute-start | bytes 1486856 | tf_op jit(solution)/shard_map/ppermute | solution.py:537
  5.2 0.7 copy-start
  10.8 5.1 %collective-permute-start.2 = (f32[2,256]{1,0:T(2,128)S(1)}, f32[2,256]{1,0:T(2,128)S(1)}, u32[]{:S(2)}, u32[]{:S(2)}) collective-permute-start(f32[2,256]{1,0:T(2,128)S(1)} %get-tuple-element.24.sums_ref), channel_id=1, source_target_pairs={{0,1},{1,0},{2,3},{3,2},{4,5},{5,4},{6,7},{7,6},{8,9},{9,8},{10,11... | collective-permute-start | bytes 6152 | tf_op jit(solution)/shard_map/ppermute | solution.py:505
  17.4 15.0 %collective-permute-start.3 = (bf16[7,44,256]{2,1,0:T(8,128)(2,1)S(1)}, bf16[7,44,256]{2,1,0:T(8,128)(2,1)S(1)}, u32[]{:S(2)}, u32[]{:S(2)}) collective-permute-start(bf16[7,44,256]{2,1,0:T(8,128)(2,1)S(1)} %get-tuple-element.27), channel_id=1, source_target_pairs={{0,16},{16,0},{32,48},{48,32},{64,80},{80,64},{96,112},{112,96},{1... | collective-permute-start | bytes 473096 | tf_op jit(solution)/shard_map/ppermute | solution.py:566
  20.3 12.2 %collective-permute-start.4 = (bf16[7,44,256]{2,1,0:T(8,128)(2,1)S(1)}, bf16[7,44,256]{2,1,0:T(8,128)(2,1)S(1)}, u32[]{:S(2)}, u32[]{:S(2)}) collective-permute-start(bf16[7,44,256]{2,1,0:T(8,128)(2,1)S(1)} %get-tuple-element.28), channel_id=1, source_target_pairs={{16,32},{32,16},{48,64},{64,48},{80,96},{96,80},{17,33},{33,17},{4... | collective-permute-start | bytes 473096 | tf_op jit(solution)/shard_map/ppermute | solution.py:567
  20.9 23.0 %all-to-all-start = ((f32[64,2,256]{2,1,0:T(2,128)}), f32[64,2,256]{2,1,0:T(2,128)S(1)}, u32[]{:S(2)}, u32[]{:S(2)}) async-start(f32[64,2,256]{2,1,0:T(2,128)} %get-tuple-element.25), calls=%async_computation | async-start | bytes 262144 | tf_op jit(solution)/shard_map/all_to_all | solution.py:509
  43.9 19.6 %copy-start.1 = (s32[22]{0:T(128)S(1)}, s32[22]{0:T(128)}, u32[]{:S(2)}) copy-start(s32[22]{0:T(128)} %reach_ref.3) | copy-start | bytes 268
  51.4 3.8 %collective-permute-start.5 = (f32[2,256]{1,0:T(2,128)S(1)}, f32[2,256]{1,0:T(2,128)S(1)}, u32[]{:S(2)}, u32[]{:S(2)}) collective-permute-start(f32[2,256]{1,0:T(2,128)S(1)} %get-tuple-element.34.sums_ref), channel_id=1, source_target_pairs={{0,1},{1,0},{2,3},{3,2},{4,5},{5,4},{6,7},{7,6},{8,9},{9,8},{10,11... | collective-permute-start | bytes 6152 | tf_op jit(solution)/shard_map/ppermute | solution.py:505
  55.8 19.3 %all-to-all-start.1 = ((f32[64,2,256]{2,1,0:T(2,128)}), f32[64,2,256]{2,1,0:T(2,128)S(1)}, u32[]{:S(2)}, u32[]{:S(2)}) async-start(f32[64,2,256]{2,1,0:T(2,128)} %shard_map.59), calls=%async_computation.1 | async-start | bytes 262144 | tf_op jit(solution)/shard_map/all_to_all | solution.py:509

commit v3 on v2

v3 whole, which is shorter than its diff:
```python
import functools
import math

import jax
import jax.numpy as jnp
import numpy as np
from jax import lax
from jax.experimental import pallas as pl
from jax.experimental.pallas import tpu as pltpu
from jax.sharding import Mesh, PartitionSpec as P

BLOCKS = 2
HMAX = 22
TAPS = 2 * HMAX + 1
TILE = 16
SPAN = 64
ROWS = 22
COLS = 44
CHANS = 256
BASIS = 9
N_LAT = 176
N_LON = 704
WIDE = 96
DEEP = BASIS * CHANS
HIGH = BASIS * TILE
LAT = ("y", "xh")
LON = ("z", "core")
F32 = jnp.float32
BF16 = jnp.bfloat16
VMEM_LIMIT = 28 * 1024 * 1024
WEIGHTS = np.cos(np.pi * (np.arange(N_LAT) + 0.5) / N_LAT - np.pi / 2)
TOTAL = float(N_LON * WEIGHTS.sum())


def lat_index():
    return lax.axis_index("y") * 2 + lax.axis_index("xh")


def area_weights(weight_ref):
    row = lax.broadcasted_iota(jnp.int32, (24, CHANS), 0)
    angle = ((lat_index() * ROWS + row).astype(F32) + 0.5) * (math.pi / N_LAT)
    weight = jnp.where(row < ROWS, jnp.sin(angle), 0.0)
    weight_ref[...] = weight
    return COLS * jnp.sum(weight, axis=0, keepdims=True)


def start_all(pairs, sems):
    copies = [pltpu.make_async_copy(s, t, sems.at[n]) for n, (s, t) in enumerate(pairs)]
    for copy in copies:
        copy.start()
    return copies


def put_band(rows, odd, store):
    halves = [None, None]
    for r in range(3):
        place = r + odd
        moved = pltpu.roll(rows[r], SPAN * (place % 2), 1, stride=1, stride_axis=0)
        half = place // 2
        halves[half] = moved if halves[half] is None else halves[half] + moved
    store(slice(0, 128), halves[0].astype(BF16))
    store(slice(128, 256), halves[1].astype(BF16))


def spread(line):
    return jnp.broadcast_to(line, (TILE, 128))


def taps_of(reach_ref, psi_ref, block, i, k, at=None):
    tap = lax.broadcasted_iota(jnp.int32, (1, TAPS), 1) - HMAX
    rest = jnp.zeros((1, 128 - TAPS), F32)
    near = jnp.abs(tap) <= reach_ref[i]
    row = lat_index() * ROWS + i - 1
    taps = []
    for r in range(3):
        keep = near & (row + r >= 0) & (row + r < N_LAT)
        line = jnp.where(keep, psi_ref[k, i if at is None else at, r].astype(F32)[block : block + 1], 0.0)
        taps.append(jnp.broadcast_to(jnp.concatenate([line, rest], axis=1), (TILE, 128)))
    return taps


def make_bands(reach_ref, psi_ref, block, band_ref, tap_sum_ref, line_ref, sends):
    def two_rows(p, _):
        for n in range(2):
            i = 2 * p + n
            for k in range(BASIS):

                def store(lanes, value):
                    band_ref[i, k * TILE : (k + 1) * TILE, lanes] = value

                rows = taps_of(reach_ref, psi_ref, block, i, k)
                put_band(rows, (n + 1 - block) % 2, store)
                line_ref[k, pl.ds(i, 1)] = (rows[0] + rows[1] + rows[2])[0:1]
        return 0

    lax.fori_loop(0, 6, two_rows, 0)
    sends[0].start()
    lax.fori_loop(6, ROWS // 2, two_rows, 0)
    sends[1].start()
    for k in range(BASIS):
        whole = jnp.sum(line_ref[k], axis=1, keepdims=True)
        tap_sum_ref[:, k * CHANS : (k + 1) * CHANS] = jnp.broadcast_to(whole, (ROWS, CHANS))


def sums_kernel(
    x_any, reach_any, psi_any, sums_ref, mean_ref, edge_ref, x_ref, reach_ref, psi_ref, weight_ref, sems
):
    ends = (0, ROWS - 1)
    reach_in, *psi_in = [
        pltpu.make_async_copy(s, t, sems.at[2 + n])
        for n, (s, t) in enumerate(
            [(reach_any, reach_ref)] + [(psi_any.at[:, i], psi_ref.at[:, n]) for n, i in enumerate(ends)]
        )
    ]
    for fetch in (reach_in, *psi_in):
        fetch.start()
    half = ROWS // 2
    parts = start_all([(x_any.at[pl.ds(n * half, half)], x_ref.at[pl.ds(n * half, half)]) for n in range(2)], sems)
    whole = area_weights(weight_ref)

    def add_row(i, carry):
        first, second = carry
        v = x_ref[i].astype(F32)
        wv = weight_ref[pl.ds(i, 1)] * v
        return first + wv, second + wv * v

    zero = jnp.zeros((COLS, CHANS), F32)
    parts[0].wait()
    carry = lax.fori_loop(0, half, add_row, (zero, zero))
    parts[1].wait()
    first, second = lax.fori_loop(half, ROWS, add_row, carry)
    first = jnp.sum(first, axis=0, keepdims=True)
    sums_ref[0:1] = first
    sums_ref[1:2] = jnp.sum(second, axis=0, keepdims=True)
    mean_ref[...] = first / whole
    for fetch in (reach_in, *psi_in):
        fetch.wait()
    for n, i in enumerate(ends):
        for k in range(BASIS):
            taps = taps_of(reach_ref, psi_ref, 0, i, k, n)
            for r in range(3):
                edge_ref[n, 3 * k + r : 3 * k + r + 1] = taps[r][0:1]


def prep_kernel(
    message_ref, reach_any, psi_any, band1_any, tap_sum1_any, band2_any, tap_sum2_any,
    reach_ref, psi_ref, band1_ref, tap_sum1_ref, band2_ref, tap_sum2_ref, line_ref, sems,
):
    psi_in, reach_in = start_all([(psi_any, psi_ref), (reach_any, reach_ref)], sems)
    psi_in.wait()
    reach_in.wait()
    outs = ((band1_ref, band1_any, tap_sum1_ref, tap_sum1_any), (band2_ref, band2_any, tap_sum2_ref, tap_sum2_any))
    half = ROWS // 2
    sends = []
    for block, (band_ref, band_any, tap_sum_ref, tap_sum_any) in enumerate(outs):
        pairs = [(band_ref.at[pl.ds(n * half, half)], band_any.at[pl.ds(n * half, half)]) for n in range(2)]
        pairs.append((tap_sum_ref, tap_sum_any))
        mine = [pltpu.make_async_copy(*pair, sems.at[3 + 3 * block + n]) for n, pair in enumerate(pairs)]
        make_bands(reach_ref, psi_ref, block, band_ref, tap_sum_ref, line_ref, mine)
        mine[2].start()
        sends += mine
    for send in sends:
        send.wait()


def message_kernel(z_ref, own_any, core_ref, edge_ref, both_ref, a_ref, b_ref, sems):
    xh = lax.axis_index("xh")
    starts = [jnp.where(xh == n, ROWS - 2, 0) for n in range(2)]
    copies = start_all(
        [(own_any.at[pl.ds(s, 2)], out.at[pl.ds(2, 2)]) for s, out in zip(starts, (a_ref, b_ref))], sems
    )
    for n, out in enumerate((a_ref, b_ref)):
        taps = jnp.where(xh == n, edge_ref[1], edge_ref[0])
        out[0:2] = z_ref[pl.ds(starts[n], 2)]
        out[4:6] = core_ref[pl.ds(starts[n], 2)]
        out[6] = jnp.zeros((COLS, CHANS), BF16)
        out[6, 0:32, 0:128] = jnp.concatenate([taps, jnp.zeros((5, 128), F32)], axis=0).astype(BF16)
    for copy in copies:
        copy.wait()


def add_kernel(sums_ref, other_ref, both_ref):
    both_ref[...] = jnp.broadcast_to((sums_ref[...] + other_ref[...])[None], both_ref.shape)


def convolve(p, band, u_ref, s_ref, tiles):
    for t in range(tiles):
        window = u_ref[pl.ds(2 * p, 4), TILE * t : TILE * t + SPAN, :].reshape(4 * SPAN, CHANS)
        s = jnp.dot(band, window, preferred_element_type=F32).astype(BF16)
        for ri in range(2):
            for k in range(BASIS):
                at = (ri * BASIS + k) * TILE
                s_ref[2 * p + ri, TILE * t : TILE * t + TILE, k * CHANS : (k + 1) * CHANS] = s[
                    at : at + TILE
                ]


def scale_of(gathered_ref, gain):
    total = jnp.sum(gathered_ref[...], axis=0)
    mean = total[0:1] / TOTAL
    scale = lax.rsqrt(total[1:2] / TOTAL - mean * mean + 1e-05) * gain
    diagonal = lax.broadcasted_iota(jnp.int32, (CHANS, CHANS), 0) == lax.broadcasted_iota(
        jnp.int32, (CHANS, CHANS), 1
    )
    return mean, jnp.sum(jnp.where(diagonal, scale, 0.0), axis=1, keepdims=True)


def scale_mixing(column, mix_ref, scaled_ref):
    for k in range(BASIS):
        scaled_ref[k * CHANS : (k + 1) * CHANS] = (mix_ref[k].astype(F32) * column).astype(BF16)


def shift_rows(tap_sum, shift, scaled_ref):
    lhs = tap_sum * jnp.concatenate([shift] * BASIS, axis=1)
    high = lhs.astype(BF16)
    low = (lhs - high.astype(F32)).astype(BF16)
    scaled = scaled_ref[...]
    return jnp.dot(high, scaled, preferred_element_type=F32) + jnp.dot(
        low, scaled, preferred_element_type=F32
    )


def first_kernel(
    local_mean_ref, a_ref, b_ref, gathered_ref, z_any, core_any, own_any, band_any, mix_any, gain_any, tap_sum_any,
    s_any, res_any, mid_ref, shift_ref, scaled_any, sums_ref, new_mean_ref,
    res_ref, mix_ref, gain_ref, tap_sum_ref, edge_sum_ref, u_ref, edge_ref, z_ref, core_ref, own_ref, band_ref,
    s_ref, scaled_ref, weight_ref, in_sems, out_sems,
):
    z_in, core_in, own_in, band_in, mix_in, gain_in, tap_in = start_all(
        [
            (z_any, z_ref),
            (core_any, core_ref),
            (own_any, own_ref),
            (band_any, band_ref),
            (mix_any.at[0], mix_ref),
            (gain_any, gain_ref),
            (tap_sum_any, tap_sum_ref),
        ],
        in_sems,
    )
    xh, core = lax.axis_index("xh"), lax.axis_index("core")
    local_mean = local_mean_ref[...]

    def put_row(r, from_z, own, from_core):
        from_z, own, from_core = from_z.astype(F32), own.astype(F32), from_core.astype(F32)
        left = jnp.where(core == 0, from_z, from_core)
        right = jnp.where(core == 0, from_core, from_z)
        pad = jnp.zeros((12, CHANS), F32)
        u_ref[r] = (jnp.concatenate([left, own, right, pad], axis=0) - local_mean).astype(BF16)
        res = jnp.concatenate([left[HMAX:], own, right[:HMAX], pad[:8]], axis=0)
        return res.astype(BF16)

    def own_row(i, _):
        res_ref[i + 1] = put_row(i + 2, z_ref[i], own_ref[i], core_ref[i])
        return 0

    z_in.wait()
    core_in.wait()
    own_in.wait()
    lax.fori_loop(0, ROWS, own_row, 0)
    band_in.wait()

    def rim(piece, upper):
        use_b = (xh == 0) if upper else (xh == 1)
        return jnp.where(use_b, b_ref[piece].astype(F32), a_ref[piece].astype(F32))

    for upper in (True, False):
        for j in range(2):
            res = put_row(
                j if upper else ROWS + 2 + j, rim(j, upper), rim(2 + j, upper), rim(4 + j, upper)
            )
            if j == (1 if upper else 0):
                res_ref[0 if upper else ROWS + 1] = res
        place = 0 if upper else 1
        lines = rim(6, upper)[:, :128]
        for k in range(BASIS):

            def store(lanes, value):
                edge_ref[place, k * TILE : (k + 1) * TILE, lanes] = value

            rows = [spread(lines[3 * k + r : 3 * k + r + 1]) for r in range(3)]
            put_band(rows, place, store)
            whole = jnp.sum((rows[0] + rows[1] + rows[2])[0:1], axis=1, keepdims=True)
            edge_sum_ref[place : place + 1, k * CHANS : (k + 1) * CHANS] = jnp.broadcast_to(
                whole, (1, CHANS)
            )

    tiles = WIDE // TILE
    def one_pair(p, _):
        band = band_ref[pl.ds(2 * p - 1, 2)].reshape(2 * HIGH, 4 * SPAN)
        convolve(p, band, u_ref, s_ref, tiles)
        return 0

    convolve(0, jnp.concatenate([edge_ref[0], band_ref[0]], axis=0), u_ref, s_ref, tiles)
    lax.fori_loop(1, ROWS // 2, one_pair, 0)
    convolve(ROWS // 2, jnp.concatenate([band_ref[ROWS - 1], edge_ref[1]], axis=0), u_ref, s_ref, tiles)

    strips = [(pl.ds(1, ROWS), pl.ds(n * (WIDE - TILE), TILE)) for n in range(2)]
    strips += [(pl.ds(n * (ROWS + 1), 1),) for n in range(2)]
    rim = start_all([(s_ref.at[at], s_any.at[at]) for at in strips] + [(res_ref, res_any)], out_sems)
    mid = 4 * TILE
    parts = (11, 11)
    spans = [(sum(parts[:g]), parts[g]) for g in range(len(parts))]
    whole = area_weights(weight_ref)
    gain_in.wait()
    mix_in.wait()
    mean, column = scale_of(gathered_ref, gain_ref[0:1])
    shift = local_mean - mean
    scale_mixing(column, mix_ref, scaled_ref)
    send_scaled = pltpu.make_async_copy(scaled_ref, scaled_any, out_sems.at[5])
    send_scaled.start()
    tap_in.wait()
    shift_ref[0:ROWS] = shift_rows(tap_sum_ref[...], shift, scaled_ref)
    shift_ref[ROWS : ROWS + 2] = shift_rows(edge_sum_ref[...], shift, scaled_ref)
    column = lax.broadcasted_iota(jnp.int32, (mid, CHANS), 0) + TILE
    mine = (column >= HMAX) & (column < HMAX + COLS)
    first = second = jnp.zeros((mid, CHANS), F32)
    for at, n in spans:
        lhs = s_ref[at + 1 : at + 1 + n, TILE : TILE + mid].reshape(n * mid, DEEP)
        conv = jnp.dot(lhs, scaled_ref[...], preferred_element_type=F32).reshape(n, mid, CHANS)
        for i in range(at, at + n):
            grown = jax.nn.gelu(conv[i - at] + shift_ref[i : i + 1])
            new = (res_ref[i + 1, TILE : TILE + mid].astype(F32) + grown).astype(BF16)
            mid_ref[i] = new
            v = jnp.where(mine, new.astype(F32), 0.0)
            wv = weight_ref[i : i + 1] * v
            first, second = first + wv, second + wv * v
    first = jnp.sum(first, axis=0, keepdims=True)
    sums_ref[0:1] = first
    sums_ref[1:2] = jnp.sum(second, axis=0, keepdims=True)
    new_mean_ref[...] = first / whole
    send_scaled.wait()
    for send in rim:
        send.wait()


def second_conv_kernel(
    mean_ref, shift_ref, mid_ref, res_any, band_any, scaled_any, s_any, mix_any,
    out_any, mix_ref, res_ref, u_ref, s_ref, rows_ref, out_ref, scaled_ref, band_ref, in_sems, out_sems,
):
    *fetches, band_in, mix_in = start_all(
        [(scaled_any, scaled_ref), (res_any, res_ref)]
        + [
            (s_any.at[pl.ds(1, ROWS), pl.ds(n * (WIDE - TILE), TILE)], s_ref.at[n])
            for n in range(2)
        ]
        + [(s_any.at[n * (ROWS + 1)], rows_ref.at[n]) for n in range(2)]
        + [(band_any, band_ref), (mix_any.at[1], mix_ref)],
        in_sems,
    )
    local_mean = mean_ref[...]

    def mid_row(i, _):
        u_ref[i + 1, TILE : 5 * TILE] = (mid_ref[i].astype(F32) - local_mean).astype(BF16)
        return 0

    lax.fori_loop(0, ROWS, mid_row, 0)

    for fetch in fetches:
        fetch.wait()
    for left in range(2):
        at = slice(left * (WIDE - TILE), left * (WIDE - TILE) + TILE)
        lhs = s_ref[left].reshape(ROWS * TILE, DEEP)
        conv = jnp.dot(lhs, scaled_ref[...], preferred_element_type=F32).reshape(ROWS, TILE, CHANS)
        for i in range(ROWS):
            grown = jax.nn.gelu(conv[i] + shift_ref[i : i + 1])
            new = (res_ref[i + 1, at].astype(F32) + grown).astype(BF16).astype(F32)
            u_ref[i + 1, at] = (new - local_mean).astype(BF16)
    lhs = rows_ref[...].reshape(2 * WIDE, DEEP)
    conv = jnp.dot(lhs, scaled_ref[...], preferred_element_type=F32).reshape(2, WIDE, CHANS)
    for n in range(2):
        e = n * (ROWS + 1)
        grown = jax.nn.gelu(conv[n] + shift_ref[ROWS + n : ROWS + n + 1])
        new = (res_ref[e].astype(F32) + grown).astype(BF16).astype(F32)
        u_ref[e] = (new - local_mean).astype(BF16)

    band_in.wait()

    def one_pair(p, _):
        band = band_ref[pl.ds(2 * p, 2)].reshape(2 * HIGH, 4 * SPAN)
        convolve(p, band, u_ref, out_ref, 3)
        send(p).start()
        return 0

    def send(p):
        at = pl.ds(2 * p, 2)
        return pltpu.make_async_copy(out_ref.at[at], out_any.at[at], out_sems.at[p])

    def end(p, _):
        send(p).wait()
        return 0

    lax.fori_loop(0, ROWS // 2, one_pair, 0)
    lax.fori_loop(0, ROWS // 2, end, 0)
    mix_in.wait()


def second_mix_kernel(
    gathered_ref, local_mean_ref, mix_ref, mid_ref, gain_any, s_any, tap_sum_any, out_any,
    gain_ref, s_ref, tap_sum_ref, scaled_ref, shift_ref, out_ref, in_sems, out_sems,
):
    cols = 3 * TILE
    parts = (4, 8, 10)
    spans = [(sum(parts[:g]), parts[g]) for g in range(len(parts))]
    gain_in, tap_in, *s_in = start_all(
        [(gain_any, gain_ref), (tap_sum_any, tap_sum_ref)]
        + [(s_any.at[pl.ds(at, n)], s_ref.at[pl.ds(at, n)]) for at, n in spans],
        in_sems,
    )
    gain_in.wait()
    mean, column = scale_of(gathered_ref, gain_ref[1:2])
    shift = local_mean_ref[...] - mean
    scale_mixing(column, mix_ref, scaled_ref)
    tap_in.wait()
    shift_ref[...] = shift_rows(tap_sum_ref[...], shift, scaled_ref)
    sends = []
    for g, (at, n) in enumerate(spans):
        s_in[g].wait()
        lhs = s_ref[at : at + n].reshape(n * cols, DEEP)
        conv = jnp.dot(lhs, scaled_ref[...], preferred_element_type=F32).reshape(n, cols, CHANS)
        for i in range(at, at + n):
            grown = jax.nn.gelu(conv[i - at] + shift_ref[i : i + 1])
            res = mid_ref[i].astype(F32)[HMAX - TILE : HMAX - TILE + COLS]
            out_ref[i] = (res + grown[:COLS]).astype(BF16)
        span = pl.ds(at, n)
        sends.append(pltpu.make_async_copy(out_ref.at[span], out_any.at[span], out_sems.at[g]))
        sends[-1].start()
    for send in sends:
        send.wait()


def shape(*dims, dtype=BF16):
    return jax.ShapeDtypeStruct(dims, dtype)


SMEM = pl.BlockSpec(memory_space=pltpu.SMEM)
VMEM = pl.BlockSpec(memory_space=pltpu.VMEM)
HBM = pl.BlockSpec(memory_space=pltpu.HBM)
KEPT = pl.BlockSpec(memory_space=pltpu.VMEM)


def call(kernel, ins, outs, scratch=(), flops=10**6):
    def out_shape(o, spec):
        space = {id(HBM): pltpu.HBM, id(KEPT): pltpu.VMEM}.get(id(spec))
        return o if space is None else space(o.shape, o.dtype)

    run = pl.pallas_call(
        kernel,
        out_shape=[out_shape(*o) for o in outs],
        in_specs=ins,
        out_specs=[spec for _, spec in outs],
        scratch_shapes=list(scratch),
        compiler_params=pltpu.CompilerParams(vmem_limit_bytes=VMEM_LIMIT),
        cost_estimate=pl.CostEstimate(flops=flops, bytes_accessed=10**6, transcendentals=0),
    )

    def in_place(v, spec):
        space = {id(HBM): pltpu.HBM, id(KEPT): pltpu.VMEM}.get(id(spec))
        return v if space is None else pltpu.with_memory_space_constraint(v, space)

    return lambda *values: run(*[in_place(v, spec) for v, spec in zip(values, ins)])


def swap_pairs(count, first):
    pairs = []
    for i in range(first, count - 1, 2):
        pairs += [(i, i + 1), (i + 1, i)]
    return pairs


def from_other_core(v):
    return lax.ppermute(v, "core", [(0, 1), (1, 0)])


def gather(both):
    return lax.all_to_all(both, ("y", "xh", "z"), 0, 0)


def buffer(*dims):
    return pltpu.VMEM(dims, BF16)


def semaphores(count):
    return pltpu.SemaphoreType.DMA((count,))


def floats(*dims):
    return pltpu.VMEM(dims, F32)


def local(x, norm_gain, mixing, kernel_psi, lon_reach):
    peers = lax.axis_size("y") * lax.axis_size("xh") * lax.axis_size("z")
    sums_out = (shape(2, CHANS, dtype=F32), VMEM)
    mean_out = (shape(1, CHANS, dtype=F32), VMEM)
    both_out = (shape(peers, 2, CHANS, dtype=F32), VMEM)
    tap_sum_out = (shape(ROWS, DEEP, dtype=F32), HBM)
    mid_cols, own_cols = 4 * TILE, 3 * TILE

    from_core = from_other_core(x)
    ring = []
    for z in range(8):
        a, b = 2 * z + 1, (2 * z + 2) % 16
        ring += [(a, b), (b, a)]
    from_z = lax.ppermute(x, LON, ring)

    psi = jnp.transpose(kernel_psi, (1, 2, 3, 0, 4))
    band_outs = [(shape(ROWS, HIGH, 4 * SPAN), HBM), tap_sum_out]
    edge_out = (shape(2, 3 * BASIS, 128, dtype=F32), VMEM)
    sums, mean, edge = call(
        sums_kernel,
        [HBM, HBM, HBM],
        [sums_out, mean_out, edge_out],
        [
            buffer(ROWS, COLS, CHANS),
            pltpu.SMEM((ROWS,), jnp.int32),
            buffer(BASIS, 2, 3, BLOCKS, TAPS),
            floats(24, CHANS),
            semaphores(5),
        ],
    )(x, lon_reach, psi)
    (both,) = call(add_kernel, [VMEM, VMEM], [both_out])(sums, from_other_core(sums))
    gathered = gather(both)

    message = (shape(7, COLS, CHANS), VMEM)
    to_a, to_b = call(message_kernel, [VMEM, HBM] + [VMEM] * 3, [message, message], [semaphores(2)])(
        from_z, x, from_core, edge, both
    )
    band1, tap_sum1, band2, tap_sum2 = call(
        prep_kernel,
        [VMEM, HBM, HBM],
        band_outs + band_outs,
        [pltpu.SMEM((ROWS,), jnp.int32), buffer(BASIS, ROWS, 3, BLOCKS, TAPS)]
        + [buffer(ROWS, HIGH, 4 * SPAN), floats(ROWS, DEEP)] * 2
        + [floats(BASIS, ROWS, 128), semaphores(9)],
        flops=5 * 10**9,
    )(to_a, lon_reach, psi)
    got_a = lax.ppermute(to_a, LAT, swap_pairs(8, 0))
    got_b = lax.ppermute(to_b, LAT, swap_pairs(8, 1))

    s1, res, mid, shift, scaled, sums1, mean1 = call(
        first_kernel,
        [VMEM] * 4 + [HBM] * 7,
        [
            (shape(ROWS + 2, WIDE, DEEP), HBM),
            (shape(ROWS + 2, WIDE, CHANS), HBM),
            (shape(ROWS, mid_cols, CHANS), KEPT),
            (shape(ROWS + 2, CHANS, dtype=F32), KEPT),
            (shape(DEEP, CHANS), HBM),
            sums_out,
            mean_out,
        ],
        [
            buffer(ROWS + 2, WIDE, CHANS),
            buffer(BASIS, CHANS, CHANS),
            floats(BLOCKS, CHANS),
            floats(ROWS, DEEP),
            floats(2, DEEP),
            buffer(ROWS + 4, 144, CHANS),
            buffer(2, HIGH, 4 * SPAN),
            buffer(ROWS, COLS, CHANS),
            buffer(ROWS, COLS, CHANS),
            buffer(ROWS, COLS, CHANS),
            buffer(ROWS, HIGH, 4 * SPAN),
            buffer(ROWS + 2, WIDE, DEEP),
            buffer(DEEP, CHANS),
            floats(24, CHANS),
            semaphores(7),
            semaphores(6),
        ],
    )(mean, got_a, got_b, gathered, from_z, from_core, x, band1, mixing, norm_gain, tap_sum1)
    (both1,) = call(add_kernel, [VMEM, VMEM], [both_out])(sums1, from_other_core(sums1))
    gathered1 = gather(both1)
    s2, mix2 = call(
        second_conv_kernel,
        [VMEM] + [KEPT] * 2 + [HBM] * 5,
        [(shape(ROWS, own_cols, DEEP), HBM), (shape(BASIS, CHANS, CHANS), KEPT)],
        [
            buffer(ROWS + 2, WIDE, CHANS),
            buffer(ROWS + 2, WIDE, CHANS),
            buffer(2, ROWS, TILE, DEEP),
            buffer(2, WIDE, DEEP),
            buffer(ROWS, own_cols, DEEP),
            buffer(DEEP, CHANS),
            buffer(ROWS, HIGH, 4 * SPAN),
            semaphores(8),
            semaphores(11),
        ],
        flops=9 * 10**9,
    )(mean1, shift, mid, res, band2, scaled, s1, mixing)
    (out,) = call(
        second_mix_kernel,
        [VMEM] * 2 + [KEPT] * 2 + [HBM] * 3,
        [(shape(ROWS, COLS, CHANS), HBM)],
        [
            floats(BLOCKS, CHANS),
            buffer(ROWS, own_cols, DEEP),
            floats(ROWS, DEEP),
            buffer(DEEP, CHANS),
            floats(ROWS, CHANS),
            buffer(ROWS, COLS, CHANS),
            semaphores(5),
            semaphores(3),
        ],
        flops=2 * 10**9,
    )(gathered1, mean1, mix2, mid, norm_gain, s2, tap_sum2)
    return out


def solution(mesh):
    split = Mesh(mesh.devices.reshape(2, 4, 2, 8, 2), ("mem", "y", "xh", "z", "core"))
    placed = (P(LAT, LON, "mem"), P(), P(), P(None, None, LAT, None, None), P(LAT))
    return jax.shard_map(
        local, mesh=split, in_specs=placed, out_specs=P(LAT, LON, "mem"), check_vma=False
    )
```

time: 82 us -> 77.9 us (0.950)
  local copies, waits for them, and re-layouts: 2.66 us -> 0.01 us
  Pallas kernels: 37.9 us -> 35.3 us
  starting transfers between devices: 33.2 us -> 35.5 us
  waiting for transfers between devices: 7.62 us -> 6.44 us
    all_to_all x2, waiting for transfers between devices: 5.97 us -> 3.29 us  [gather(): return lax.all_to_all(both, ('y', 'xh', 'z'), 0, 0)]
    pallas_call x7 -> x8, Pallas kernels: 37.9 us -> 35.3 us  [call(): run(*[in_place(v, spec) for v, spec in zip(values, ins)])]
    ppermute x1, starting transfers between devices: 2.83 us -> 5.03 us  [local(): got_a = lax.ppermute(to_a, LAT, swap_pairs(8, 0))]
    pad x1 -> x0, local copies, waits for them, and re-layouts: 2 us -> none  [local(): psi = jnp.pad(psi, ((0, 0),) * 4 + ((0, 128 - TAPS),))]
    all_to_all x2, starting transfers between devices: 19.2 us -> 20.7 us  [gather(): return lax.all_to_all(both, ('y', 'xh', 'z'), 0, 0)]
    ppermute x1, waiting for transfers between devices: 0.01 us -> 1.5 us  [local(): got_a = lax.ppermute(to_a, LAT, swap_pairs(8, 0))]
    ppermute x3, starting transfers between devices: 10.5 us -> 9.12 us  [from_other_core(): return lax.ppermute(v, 'core', [(0, 1), (1, 0)])]
  transfers between devices with their start and end apart: 8 -> 8, of which waited for: 4 -> 4; matrix products, arithmetic and copies ran while one was open for 2% -> 0% of each run, Pallas kernels for 27% -> 24%
where the time goes in v3:
time: 77.9 us; the launch traced here: 77.5 us
  starting transfers between devices  35.5 us (46%)
  Pallas kernels  35.3 us (45%)
  waiting for transfers between devices  6.44 us (8%)
    pallas_call x8, Pallas kernels, call(): run(*[in_place(v, spec) for v, spec in zip(values, ins)])  35.3 us
    all_to_all x2, starting transfers between devices, gather(): return lax.all_to_all(both, ('y', 'xh', 'z'), 0, 0)  20.7 us
    ppermute x3, starting transfers between devices, from_other_core(): return lax.ppermute(v, 'core', [(0, 1), (1, 0)])  9.12 us
    ppermute x1, starting transfers between devices, local(): got_a = lax.ppermute(to_a, LAT, swap_pairs(8, 0))  5.03 us
    all_to_all x2, waiting for transfers between devices, gather(): return lax.all_to_all(both, ('y', 'xh', 'z'), 0, 0)  3.29 us
    ppermute x3, waiting for transfers between devices, from_other_core(): return lax.ppermute(v, 'core', [(0, 1), (1, 0)])  1.64 us
  transfers between devices with their start and end apart: 8, of which 4 were waited for; matrix products, arithmetic and copies ran while one was open for 0% of the time, Pallas kernels for 24%

profile of v3, /device:TPU:1, one launch (start us, length us, event | category | flops | bytes accessed | tf_op | source)
XLA Modules:
  0.0 77.5 jit_solution(8580589190463381578)
XLA Ops:
  0.0 3.2 %collective-permute-start.1 = (bf16[22,44,256]{2,1,0:T(8,128)(2,1)}, bf16[22,44,256]{2,1,0:T(8,128)(2,1)S(1)}, u32[]{:S(2)}, u32[]{:S(2)}) collective-permute-start(bf16[22,44,256]{2,1,0:T(8,128)(2,1)} %own_any.3), channel_id=1, source_target_pairs={{0,1},{1,0},{2,3},{3,2},{4,5},{5,4},{6,7},{7,6},{8,9},{9,8},{10,11... | collective-permute-start | bytes 1486856 | tf_op jit(solution)/shard_map/ppermute | solution.py:472
  3.2 0.0 collective-permute-start
  3.2 1.4 %shard_map.55 = (f32[2,256]{1,0:T(2,128)S(1)}, f32[1,256]{1,0:T(1,128)S(1)}, f32[2,27,128]{2,1,0:T(8,128)S(1)}) custom-call(bf16[22,44,256]{2,1,0:T(8,128)(2,1)} %own_any.3, s32[22]{0:T(128)} %reach_any.3, bf16[9,22,3,2,45]{4,3,2,1,0:T(2,128)(2,1)} %bitcast.1), custom_call_target="tpu_custom_call" | custom-call | flops 1000000 | bytes 1000000 | tf_op jit(solution)/shard_map/pallas_call | solution.py:461
  4.7 4.3 %collective-permute-start.2 = (f32[2,256]{1,0:T(2,128)S(1)}, f32[2,256]{1,0:T(2,128)S(1)}, u32[]{:S(2)}, u32[]{:S(2)}) collective-permute-start(f32[2,256]{1,0:T(2,128)S(1)} %get-tuple-element.25.sums_ref), channel_id=1, source_target_pairs={{0,1},{1,0},{2,3},{3,2},{4,5},{5,4},{6,7},{7,6},{8,9},{9,8},{10,11... | collective-permute-start | bytes 6152 | tf_op jit(solution)/shard_map/ppermute | solution.py:472
  9.0 0.8 %collective-permute-done.2.other_ref = f32[2,256]{1,0:T(2,128)S(1)} collective-permute-done((f32[2,256]{1,0:T(2,128)S(1)}, f32[2,256]{1,0:T(2,128)S(1)}, u32[]{:S(2)}, u32[]{:S(2)}) %collective-permute-start.2) | collective-permute-done | bytes 2080 | tf_op jit(solution)/shard_map/ppermute | solution.py:472
  9.8 0.7 shard_map.56.both_ref
  10.5 9.3 %all-to-all-start = ((f32[64,2,256]{2,1,0:T(2,128)}), f32[64,2,256]{2,1,0:T(2,128)S(1)}, u32[]{:S(2)}, u32[]{:S(2)}) async-start(f32[64,2,256]{2,1,0:T(2,128)} %shard_map.56.both_ref), calls=%async_computation | async-start | bytes 262144 | tf_op jit(solution)/shard_map/all_to_all | solution.py:476
  19.8 0.0 collective-permute-done.1.core_ref.core_any
  19.8 0.0 collective-permute-done.z_ref.z_any
  19.8 0.0 copy-start.1
  19.8 1.9 %shard_map.57 = (bf16[7,44,256]{2,1,0:T(8,128)(2,1)S(1)}, bf16[7,44,256]{2,1,0:T(8,128)(2,1)S(1)}) custom-call(bf16[22,44,256]{2,1,0:T(8,128)(2,1)S(1)} %collective-permute-done.z_ref.z_any, bf16[22,44,256]{2,1,0:T(8,128)(2,1)} %own_any.3, bf16[22,44,256]{2,1,0:T(8,128)(2,1)S(1)} %collective-permute-done.1.core_ref.core_any, ...), custom_call_target="tpu_custom_call" | custom-call | flops 1000000 | bytes 1000000 | tf_op jit(solution)/shard_map/pallas_call | solution.py:461
  21.7 0.7 collective-permute-start.4
  22.4 5.0 %collective-permute-start.3 = (bf16[7,44,256]{2,1,0:T(8,128)(2,1)S(1)}, bf16[7,44,256]{2,1,0:T(8,128)(2,1)S(1)}, u32[]{:S(2)}, u32[]{:S(2)}) collective-permute-start(bf16[7,44,256]{2,1,0:T(8,128)(2,1)S(1)} %get-tuple-element.26.message_ref), channel_id=1, source_target_pairs={{0,16},{16,0},{32,48},{48,32},{64,80},{80,64},{96,112},{112,96},{1... | collective-permute-start | bytes 473096 | tf_op jit(solution)/shard_map/ppermute | solution.py:537
  27.4 6.1 %shard_map.58 = (bf16[22,144,256]{2,1,0:T(8,128)(2,1)}, f32[22,2304]{1,0:T(8,128)}, bf16[22,144,256]{2,1,0:T(8,128)(2,1)}, f32[22,2304]{1,0:T(8,128)}) custom-call(bf16[7,44,256]{2,1,0:T(8,128)(2,1)S(1)} %get-tuple-element.26.message_ref, s32[22]{0:T(128)} %reach_any.3, bf16[9,22,3,2,45]{4,3,2,1,0:T(2,128)(2,1)} %bitcast.2), custom_call_target="tpu_custom_call" | custom-call | flops 5000000000 | bytes 1000000 | tf_op jit(solution)/shard_map/pallas_call | solution.py:461
  33.6 0.0 all-to-all-done.gathered_ref
  33.6 1.5 %collective-permute-done.3.a_ref = bf16[7,44,256]{2,1,0:T(8,128)(2,1)S(1)} collective-permute-done((bf16[7,44,256]{2,1,0:T(8,128)(2,1)S(1)}, bf16[7,44,256]{2,1,0:T(8,128)(2,1)S(1)}, u32[]{:S(2)}, u32[]{:S(2)}) %collective-permute-start.3) | collective-permute-done | bytes 157728 | tf_op jit(solution)/shard_map/ppermute | solution.py:537
  35.1 10.5 %shard_map.59 = (bf16[24,96,2304]{2,1,0:T(8,128)(2,1)}, bf16[24,96,256]{2,1,0:T(8,128)(2,1)}, bf16[22,64,256]{2,1,0:T(8,128)(2,1)S(1)}, f32[24,256]{1,0:T(8,128)...) custom-call(f32[1,256]{1,0:T(1,128)S(1)} %get-tuple-element.23.local_mean_ref, ...), custom_call_target="tpu_custom_call" | custom-call | flops 1000000 | bytes 1000000 | tf_op jit(solution)/shard_map/pallas_call | solution.py:461
  45.6 1.6 %collective-permute-start.5 = (f32[2,256]{1,0:T(2,128)S(1)}, f32[2,256]{1,0:T(2,128)S(1)}, u32[]{:S(2)}, u32[]{:S(2)}) collective-permute-start(f32[2,256]{1,0:T(2,128)S(1)} %get-tuple-element.30.sums_ref), channel_id=1, source_target_pairs={{0,1},{1,0},{2,3},{3,2},{4,5},{5,4},{6,7},{7,6},{8,9},{9,8},{10,11... | collective-permute-start | bytes 6152 | tf_op jit(solution)/shard_map/ppermute | solution.py:472
  47.2 0.8 %collective-permute-done.5.other_ref = f32[2,256]{1,0:T(2,128)S(1)} collective-permute-done((f32[2,256]{1,0:T(2,128)S(1)}, f32[2,256]{1,0:T(2,128)S(1)}, u32[]{:S(2)}, u32[]{:S(2)}) %collective-permute-start.5) | collective-permute-done | bytes 2080 | tf_op jit(solution)/shard_map/ppermute | solution.py:472
  48.0 0.7 shard_map.60
  48.7 11.4 %all-to-all-start.1 = ((f32[64,2,256]{2,1,0:T(2,128)}), f32[64,2,256]{2,1,0:T(2,128)S(1)}, u32[]{:S(2)}, u32[]{:S(2)}) async-start(f32[64,2,256]{2,1,0:T(2,128)} %shard_map.60), calls=%async_computation.1 | async-start | bytes 262144 | tf_op jit(solution)/shard_map/all_to_all | solution.py:476
  60.1 8.3 %shard_map.61 = (bf16[22,48,2304]{2,1,0:T(8,128)(2,1)}, bf16[9,256,256]{2,1,0:T(8,128)(2,1)S(1)}) custom-call(f32[1,256]{1,0:T(1,128)S(1)} %get-tuple-element.31.mean_ref.local_mean_ref, f32[24,256]{1,0:T(8,128)S(1)} %get-tuple-element.32.shift_ref, bf16[22,64,256]{2,1,0:T(8,128)(2,1)S(1)} %get-tuple-element.33.mid_ref, ...), custom_call_target="tpu_custom_call" | custom-call | flops 8999999488 | bytes 1000000 | tf_op jit(solution)/shard_map/pallas_call | solution.py:461
  68.4 3.3 %all-to-all-done.1.gathered_ref = f32[64,2,256]{2,1,0:T(2,128)S(1)} async-done(((f32[64,2,256]{2,1,0:T(2,128)}), f32[64,2,256]{2,1,0:T(2,128)S(1)}, u32[]{:S(2)}, u32[]{:S(2)}) %all-to-all-start.1) | async-done | bytes 131104 | tf_op jit(solution)/shard_map/all_to_all | solution.py:476
  71.7 5.7 %shard_map.62 = bf16[22,44,256]{2,1,0:T(8,128)(2,1)} custom-call(f32[64,2,256]{2,1,0:T(2,128)S(1)} %all-to-all-done.1.gathered_ref, f32[1,256]{1,0:T(1,128)S(1)} %get-tuple-element.31.mean_ref.local_mean_ref, bf16[9,256,256]{2,1,0:T(8,128)(2,1)S(1)} %get-tuple-element.38.mix_ref, bf16[22,64,256]{2,1,0:T(8,128)(2,1)S(1)} %get-tuple-element.33.mid_ref, ...), custom_call_target="tpu_custom_call" | custom-call | flops 2000000000 | bytes 1000000 | tf_op jit(solution)/shard_map/pallas_call | solution.py:461
  (4 shorter events, 0.0 us)
Async XLA Ops:
  0.0 19.8 %collective-permute-start.1 = (bf16[22,44,256]{2,1,0:T(8,128)(2,1)}, bf16[22,44,256]{2,1,0:T(8,128)(2,1)S(1)}, u32[]{:S(2)}, u32[]{:S(2)}) collective-permute-start(bf16[22,44,256]{2,1,0:T(8,128)(2,1)} %own_any.3), channel_id=1, source_target_pairs={{0,1},{1,0},{2,3},{3,2},{4,5},{5,4},{6,7},{7,6},{8,9},{9,8},{10,11... | collective-permute-start | bytes 1486856 | tf_op jit(solution)/shard_map/ppermute | solution.py:472
  3.2 16.6 %collective-permute-start = (bf16[22,44,256]{2,1,0:T(8,128)(2,1)}, bf16[22,44,256]{2,1,0:T(8,128)(2,1)S(1)}, u32[]{:S(2)}, u32[]{:S(2)}) collective-permute-start(bf16[22,44,256]{2,1,0:T(8,128)(2,1)} %own_any.3), channel_id=1, source_target_pairs={{1,2},{2,1},{3,4},{4,3},{5,6},{6,5},{7,8},{8,7},{9,10},{10,9},{11,... | collective-permute-start | bytes 1486856 | tf_op jit(solution)/shard_map/ppermute | solution.py:504
  4.7 5.1 %collective-permute-start.2 = (f32[2,256]{1,0:T(2,128)S(1)}, f32[2,256]{1,0:T(2,128)S(1)}, u32[]{:S(2)}, u32[]{:S(2)}) collective-permute-start(f32[2,256]{1,0:T(2,128)S(1)} %get-tuple-element.25.sums_ref), channel_id=1, source_target_pairs={{0,1},{1,0},{2,3},{3,2},{4,5},{5,4},{6,7},{7,6},{8,9},{9,8},{10,11... | collective-permute-start | bytes 6152 | tf_op jit(solution)/shard_map/ppermute | solution.py:472
  10.5 23.1 %all-to-all-start = ((f32[64,2,256]{2,1,0:T(2,128)}), f32[64,2,256]{2,1,0:T(2,128)S(1)}, u32[]{:S(2)}, u32[]{:S(2)}) async-start(f32[64,2,256]{2,1,0:T(2,128)} %shard_map.56.both_ref), calls=%async_computation | async-start | bytes 262144 | tf_op jit(solution)/shard_map/all_to_all | solution.py:476
  19.8 13.8 %copy-start = (bf16[22,44,256]{2,1,0:T(8,128)(2,1)}, bf16[22,44,256]{2,1,0:T(8,128)(2,1)S(1)}, u32[]{:S(2)}) copy-start(bf16[22,44,256]{2,1,0:T(8,128)(2,1)S(1)} %collective-permute-done.1.core_ref.core_any) | copy-start | bytes 1486852
  19.8 13.8 %copy-start.1 = (bf16[22,44,256]{2,1,0:T(8,128)(2,1)}, bf16[22,44,256]{2,1,0:T(8,128)(2,1)S(1)}, u32[]{:S(2)}) copy-start(bf16[22,44,256]{2,1,0:T(8,128)(2,1)S(1)} %collective-permute-done.z_ref.z_any) | copy-start | bytes 1486852
  21.7 11.9 %collective-permute-start.4 = (bf16[7,44,256]{2,1,0:T(8,128)(2,1)S(1)}, bf16[7,44,256]{2,1,0:T(8,128)(2,1)S(1)}, u32[]{:S(2)}, u32[]{:S(2)}) collective-permute-start(bf16[7,44,256]{2,1,0:T(8,128)(2,1)S(1)} %get-tuple-element.27), channel_id=1, source_target_pairs={{16,32},{32,16},{48,64},{64,48},{80,96},{96,80},{17,33},{33,17},{4... | collective-permute-start | bytes 473096 | tf_op jit(solution)/shard_map/ppermute | solution.py:538
  22.4 12.7 %collective-permute-start.3 = (bf16[7,44,256]{2,1,0:T(8,128)(2,1)S(1)}, bf16[7,44,256]{2,1,0:T(8,128)(2,1)S(1)}, u32[]{:S(2)}, u32[]{:S(2)}) collective-permute-start(bf16[7,44,256]{2,1,0:T(8,128)(2,1)S(1)} %get-tuple-element.26.message_ref), channel_id=1, source_target_pairs={{0,16},{16,0},{32,48},{48,32},{64,80},{80,64},{96,112},{112,96},{1... | collective-permute-start | bytes 473096 | tf_op jit(solution)/shard_map/ppermute | solution.py:537
  45.6 2.4 %collective-permute-start.5 = (f32[2,256]{1,0:T(2,128)S(1)}, f32[2,256]{1,0:T(2,128)S(1)}, u32[]{:S(2)}, u32[]{:S(2)}) collective-permute-start(f32[2,256]{1,0:T(2,128)S(1)} %get-tuple-element.30.sums_ref), channel_id=1, source_target_pairs={{0,1},{1,0},{2,3},{3,2},{4,5},{5,4},{6,7},{7,6},{8,9},{9,8},{10,11... | collective-permute-start | bytes 6152 | tf_op jit(solution)/shard_map/ppermute | solution.py:472
  48.7 23.0 %all-to-all-start.1 = ((f32[64,2,256]{2,1,0:T(2,128)}), f32[64,2,256]{2,1,0:T(2,128)S(1)}, u32[]{:S(2)}, u32[]{:S(2)}) async-start(f32[64,2,256]{2,1,0:T(2,128)} %shard_map.60), calls=%async_computation.1 | async-start | bytes 262144 | tf_op jit(solution)/shard_map/all_to_all | solution.py:476

commit v4 on v3

--- a/solution.py
+++ b/solution.py
@@ -222,22 +222,21 @@
 
 def first_kernel(
     local_mean_ref, a_ref, b_ref, gathered_ref, z_any, core_any, own_any, band_any, mix_any, gain_any, tap_sum_any,
-    s_any, res_any, mid_ref, shift_ref, scaled_any, sums_ref, new_mean_ref,
+    s_any, res_any, mid_ref, shift_ref, scaled_ref, sums_ref, new_mean_ref,
     res_ref, mix_ref, gain_ref, tap_sum_ref, edge_sum_ref, u_ref, edge_ref, z_ref, core_ref, own_ref, band_ref,
-    s_ref, scaled_ref, weight_ref, in_sems, out_sems,
+    s_ref, weight_ref, in_sems, out_sems,
 ):
-    z_in, core_in, own_in, band_in, mix_in, gain_in, tap_in = start_all(
-        [
-            (z_any, z_ref),
-            (core_any, core_ref),
-            (own_any, own_ref),
-            (band_any, band_ref),
-            (mix_any.at[0], mix_ref),
-            (gain_any, gain_ref),
-            (tap_sum_any, tap_sum_ref),
-        ],
-        in_sems,
-    )
+    z_in, core_in, own_in = start_all(
+        [(z_any, z_ref), (core_any, core_ref), (own_any, own_ref)], in_sems
+    )
+    pairs = (
+        (band_any, band_ref),
+        (mix_any.at[0], mix_ref),
+        (gain_any, gain_ref),
+        (tap_sum_any, tap_sum_ref),
+    )
+    later = [pltpu.make_async_copy(s, t, in_sems.at[3 + n]) for n, (s, t) in enumerate(pairs)]
+    band_in, mix_in, gain_in, tap_in = later
     xh, core = lax.axis_index("xh"), lax.axis_index("core")
     local_mean = local_mean_ref[...]
 
@@ -257,6 +256,8 @@
     z_in.wait()
     core_in.wait()
     own_in.wait()
+    for fetch in later:
+        fetch.start()
     lax.fori_loop(0, ROWS, own_row, 0)
     band_in.wait()
 
@@ -307,8 +308,6 @@
     mean, column = scale_of(gathered_ref, gain_ref[0:1])
     shift = local_mean - mean
     scale_mixing(column, mix_ref, scaled_ref)
-    send_scaled = pltpu.make_async_copy(scaled_ref, scaled_any, out_sems.at[5])
-    send_scaled.start()
     tap_in.wait()
     shift_ref[0:ROWS] = shift_rows(tap_sum_ref[...], shift, scaled_ref)
     shift_ref[ROWS : ROWS + 2] = shift_rows(edge_sum_ref[...], shift, scaled_ref)
@@ -329,25 +328,24 @@
     sums_ref[0:1] = first
     sums_ref[1:2] = jnp.sum(second, axis=0, keepdims=True)
     new_mean_ref[...] = first / whole
-    send_scaled.wait()
     for send in rim:
         send.wait()
 
 
 def second_conv_kernel(
-    mean_ref, shift_ref, mid_ref, res_any, band_any, scaled_any, s_any, mix_any,
-    out_any, mix_ref, res_ref, u_ref, s_ref, rows_ref, out_ref, scaled_ref, band_ref, in_sems, out_sems,
+    mean_ref, shift_ref, mid_ref, scaled_ref, res_any, band_any, s_any, mix_any,
+    out_any, mix_ref, res_ref, u_ref, s_ref, rows_ref, out_ref, band_ref, in_sems, out_sems,
 ):
-    *fetches, band_in, mix_in = start_all(
-        [(scaled_any, scaled_ref), (res_any, res_ref)]
-        + [
-            (s_any.at[pl.ds(1, ROWS), pl.ds(n * (WIDE - TILE), TILE)], s_ref.at[n])
-            for n in range(2)
-        ]
-        + [(s_any.at[n * (ROWS + 1)], rows_ref.at[n]) for n in range(2)]
-        + [(band_any, band_ref), (mix_any.at[1], mix_ref)],
+    strips = [(pl.ds(1, ROWS), pl.ds(n * (WIDE - TILE), TILE)) for n in range(2)]
+    edges = [n * (ROWS + 1) for n in range(2)]
+    fetches = start_all(
+        [(s_any.at[at], s_ref.at[n]) for n, at in enumerate(strips)]
+        + [(s_any.at[at], rows_ref.at[n]) for n, at in enumerate(edges)]
+        + [(res_any.at[at], res_ref.at[at]) for at in strips + edges],
         in_sems,
     )
+    band_in = pltpu.make_async_copy(band_any, band_ref, in_sems.at[8])
+    mix_in = pltpu.make_async_copy(mix_any.at[1], mix_ref, in_sems.at[9])
     local_mean = mean_ref[...]
 
     def mid_row(i, _):
@@ -358,6 +356,8 @@
 
     for fetch in fetches:
         fetch.wait()
+    band_in.start()
+    mix_in.start()
     for left in range(2):
         at = slice(left * (WIDE - TILE), left * (WIDE - TILE) + TILE)
         lhs = s_ref[left].reshape(ROWS * TILE, DEEP)
@@ -545,7 +545,7 @@
             (shape(ROWS + 2, WIDE, CHANS), HBM),
             (shape(ROWS, mid_cols, CHANS), KEPT),
             (shape(ROWS + 2, CHANS, dtype=F32), KEPT),
-            (shape(DEEP, CHANS), HBM),
+            (shape(DEEP, CHANS), KEPT),
             sums_out,
             mean_out,
         ],
@@ -562,17 +562,16 @@
             buffer(ROWS, COLS, CHANS),
             buffer(ROWS, HIGH, 4 * SPAN),
             buffer(ROWS + 2, WIDE, DEEP),
-            buffer(DEEP, CHANS),
             floats(24, CHANS),
             semaphores(7),
-            semaphores(6),
+            semaphores(5),
         ],
     )(mean, got_a, got_b, gathered, from_z, from_core, x, band1, mixing, norm_gain, tap_sum1)
     (both1,) = call(add_kernel, [VMEM, VMEM], [both_out])(sums1, from_other_core(sums1))
     gathered1 = gather(both1)
     s2, mix2 = call(
         second_conv_kernel,
-        [VMEM] + [KEPT] * 2 + [HBM] * 5,
+        [VMEM] + [KEPT] * 3 + [HBM] * 4,
         [(shape(ROWS, own_cols, DEEP), HBM), (shape(BASIS, CHANS, CHANS), KEPT)],
         [
             buffer(ROWS + 2, WIDE, CHANS),
@@ -580,13 +579,12 @@
             buffer(2, ROWS, TILE, DEEP),
             buffer(2, WIDE, DEEP),
             buffer(ROWS, own_cols, DEEP),
-            buffer(DEEP, CHANS),
             buffer(ROWS, HIGH, 4 * SPAN),
-            semaphores(8),
+            semaphores(10),
             semaphores(11),
         ],
         flops=9 * 10**9,
-    )(mean1, shift, mid, res, band2, scaled, s1, mixing)
+    )(mean1, shift, mid, scaled, res, band2, s1, mixing)
     (out,) = call(
         second_mix_kernel,
         [VMEM] * 2 + [KEPT] * 2 + [HBM] * 3,

time: 77.9 us -> 79.6 us (1.022)
  local copies, waits for them, and re-layouts: 0.01 us -> 2.29 us
    unnamed x4 -> x8, local copies, waits for them, and re-layouts: 0.01 us -> 2.29 us
  transfers between devices with their start and end apart: 8 -> 8, of which waited for: 4 -> 4; matrix products, arithmetic and copies ran while one was open for 0% -> 0% of each run, Pallas kernels for 24% -> 22%
where the time goes in v4:
time: 79.6 us; the launch traced here: 79.2 us
  starting transfers between devices  35.4 us (44%)
  Pallas kernels  35.4 us (44%)
  waiting for transfers between devices  5.74 us (7%)
  local copies, waits for them, and re-layouts  2.29 us (3%)
    pallas_call x8, Pallas kernels, call(): run(*[in_place(v, spec) for v, spec in zip(values, ins)])  35.4 us
    all_to_all x2, starting transfers between devices, gather(): return lax.all_to_all(both, ('y', 'xh', 'z'), 0, 0)  20.7 us
    ppermute x3, starting transfers between devices, from_other_core(): return lax.ppermute(v, 'core', [(0, 1), (1, 0)])  9.02 us
    ppermute x1, starting transfers between devices, local(): got_a = lax.ppermute(to_a, LAT, swap_pairs(8, 0))  5.03 us
    all_to_all x2, waiting for transfers between devices, gather(): return lax.all_to_all(both, ('y', 'xh', 'z'), 0, 0)  2.57 us
    unnamed x8, local copies, waits for them, and re-layouts  2.29 us
    ppermute x3, waiting for transfers between devices, from_other_core(): return lax.ppermute(v, 'core', [(0, 1), (1, 0)])  1.64 us
  transfers between devices with their start and end apart: 8, of which 4 were waited for; matrix products, arithmetic and copies ran while one was open for 0% of the time, Pallas kernels for 22%

profile of v4, /device:TPU:1, one launch (start us, length us, event | category | flops | bytes accessed | tf_op | source)
XLA Modules:
  0.0 79.2 jit_solution(10886150876354645038)
XLA Ops:
  0.0 3.2 %collective-permute-start.1 = (bf16[22,44,256]{2,1,0:T(8,128)(2,1)}, bf16[22,44,256]{2,1,0:T(8,128)(2,1)S(1)}, u32[]{:S(2)}, u32[]{:S(2)}) collective-permute-start(bf16[22,44,256]{2,1,0:T(8,128)(2,1)} %own_any.3), channel_id=1, source_target_pairs={{0,1},{1,0},{2,3},{3,2},{4,5},{5,4},{6,7},{7,6},{8,9},{9,8},{10,11... | collective-permute-start | bytes 1486856 | tf_op jit(solution)/shard_map/ppermute | solution.py:472
  3.2 0.0 collective-permute-start
  3.2 1.4 %shard_map.55 = (f32[2,256]{1,0:T(2,128)S(1)}, f32[1,256]{1,0:T(1,128)S(1)}, f32[2,27,128]{2,1,0:T(8,128)S(1)}) custom-call(bf16[22,44,256]{2,1,0:T(8,128)(2,1)} %own_any.3, s32[22]{0:T(128)} %reach_any.3, bf16[9,22,3,2,45]{4,3,2,1,0:T(2,128)(2,1)} %bitcast.1), custom_call_target="tpu_custom_call" | custom-call | flops 1000000 | bytes 1000000 | tf_op jit(solution)/shard_map/pallas_call | solution.py:461
  4.7 4.3 %collective-permute-start.2 = (f32[2,256]{1,0:T(2,128)S(1)}, f32[2,256]{1,0:T(2,128)S(1)}, u32[]{:S(2)}, u32[]{:S(2)}) collective-permute-start(f32[2,256]{1,0:T(2,128)S(1)} %get-tuple-element.25.sums_ref), channel_id=1, source_target_pairs={{0,1},{1,0},{2,3},{3,2},{4,5},{5,4},{6,7},{7,6},{8,9},{9,8},{10,11... | collective-permute-start | bytes 6152 | tf_op jit(solution)/shard_map/ppermute | solution.py:472
  9.0 0.8 %collective-permute-done.2.other_ref = f32[2,256]{1,0:T(2,128)S(1)} collective-permute-done((f32[2,256]{1,0:T(2,128)S(1)}, f32[2,256]{1,0:T(2,128)S(1)}, u32[]{:S(2)}, u32[]{:S(2)}) %collective-permute-start.2) | collective-permute-done | bytes 2080 | tf_op jit(solution)/shard_map/ppermute | solution.py:472
  9.8 0.7 shard_map.56.both_ref
  10.5 9.3 %all-to-all-start = ((f32[64,2,256]{2,1,0:T(2,128)}), f32[64,2,256]{2,1,0:T(2,128)S(1)}, u32[]{:S(2)}, u32[]{:S(2)}) async-start(f32[64,2,256]{2,1,0:T(2,128)} %shard_map.56.both_ref), calls=%async_computation | async-start | bytes 262144 | tf_op jit(solution)/shard_map/all_to_all | solution.py:476
  19.8 0.0 collective-permute-done.1.core_ref.core_any
  19.8 0.0 copy-start.1
  19.8 1.9 %shard_map.57 = (bf16[7,44,256]{2,1,0:T(8,128)(2,1)S(1)}, bf16[7,44,256]{2,1,0:T(8,128)(2,1)S(1)}) custom-call(bf16[22,44,256]{2,1,0:T(8,128)(2,1)S(1)} %collective-permute-done.z_ref.z_any, bf16[22,44,256]{2,1,0:T(8,128)(2,1)} %own_any.3, bf16[22,44,256]{2,1,0:T(8,128)(2,1)S(1)} %collective-permute-done.1.core_ref.core_any, ...), custom_call_target="tpu_custom_call" | custom-call | flops 1000000 | bytes 1000000 | tf_op jit(solution)/shard_map/pallas_call | solution.py:461
  21.7 0.7 collective-permute-start.4
  22.4 5.0 %collective-permute-start.3 = (bf16[7,44,256]{2,1,0:T(8,128)(2,1)S(1)}, bf16[7,44,256]{2,1,0:T(8,128)(2,1)S(1)}, u32[]{:S(2)}, u32[]{:S(2)}) collective-permute-start(bf16[7,44,256]{2,1,0:T(8,128)(2,1)S(1)} %get-tuple-element.26.message_ref), channel_id=1, source_target_pairs={{0,16},{16,0},{32,48},{48,32},{64,80},{80,64},{96,112},{112,96},{1... | collective-permute-start | bytes 473096 | tf_op jit(solution)/shard_map/ppermute | solution.py:537
  27.4 6.1 %shard_map.58 = (bf16[22,144,256]{2,1,0:T(8,128)(2,1)}, f32[22,2304]{1,0:T(8,128)}, bf16[22,144,256]{2,1,0:T(8,128)(2,1)}, f32[22,2304]{1,0:T(8,128)}) custom-call(bf16[7,44,256]{2,1,0:T(8,128)(2,1)S(1)} %get-tuple-element.26.message_ref, s32[22]{0:T(128)} %reach_any.3, bf16[9,22,3,2,45]{4,3,2,1,0:T(2,128)(2,1)} %bitcast.2), custom_call_target="tpu_custom_call" | custom-call | flops 5000000000 | bytes 1000000 | tf_op jit(solution)/shard_map/pallas_call | solution.py:461
  33.5 1.5 %collective-permute-done.3.a_ref = bf16[7,44,256]{2,1,0:T(8,128)(2,1)S(1)} collective-permute-done((bf16[7,44,256]{2,1,0:T(8,128)(2,1)S(1)}, bf16[7,44,256]{2,1,0:T(8,128)(2,1)S(1)}, u32[]{:S(2)}, u32[]{:S(2)}) %collective-permute-start.3) | collective-permute-done | bytes 157728 | tf_op jit(solution)/shard_map/ppermute | solution.py:537
  35.1 11.3 %shard_map.59 = (bf16[24,96,2304]{2,1,0:T(8,128)(2,1)}, bf16[24,96,256]{2,1,0:T(8,128)(2,1)}, bf16[22,64,256]{2,1,0:T(8,128)(2,1)S(1)}, f32[24,256]{1,0:T(8,128)...) custom-call(f32[1,256]{1,0:T(1,128)S(1)} %get-tuple-element.23.local_mean_ref, ...), custom_call_target="tpu_custom_call" | custom-call | flops 1000000 | bytes 1000000 | tf_op jit(solution)/shard_map/pallas_call | solution.py:461
  46.4 1.0 %copy-done.2 = bf16[2304,256]{1,0:T(8,128)(2,1)} copy-done((bf16[2304,256]{1,0:T(8,128)(2,1)}, bf16[2304,256]{1,0:T(8,128)(2,1)S(1)}, u32[]{:S(2)}) %copy-start.2) | copy-done | bytes 1179672
  47.4 1.5 %collective-permute-start.5 = (f32[2,256]{1,0:T(2,128)S(1)}, f32[2,256]{1,0:T(2,128)S(1)}, u32[]{:S(2)}, u32[]{:S(2)}) collective-permute-start(f32[2,256]{1,0:T(2,128)S(1)} %get-tuple-element.30.sums_ref), channel_id=1, source_target_pairs={{0,1},{1,0},{2,3},{3,2},{4,5},{5,4},{6,7},{7,6},{8,9},{9,8},{10,11... | collective-permute-start | bytes 6152 | tf_op jit(solution)/shard_map/ppermute | solution.py:472
  48.8 0.8 %collective-permute-done.5.other_ref = f32[2,256]{1,0:T(2,128)S(1)} collective-permute-done((f32[2,256]{1,0:T(2,128)S(1)}, f32[2,256]{1,0:T(2,128)S(1)}, u32[]{:S(2)}, u32[]{:S(2)}) %collective-permute-start.5) | collective-permute-done | bytes 2080 | tf_op jit(solution)/shard_map/ppermute | solution.py:472
  49.7 0.7 shard_map.60
  50.3 11.4 %all-to-all-start.1 = ((f32[64,2,256]{2,1,0:T(2,128)}), f32[64,2,256]{2,1,0:T(2,128)S(1)}, u32[]{:S(2)}, u32[]{:S(2)}) async-start(f32[64,2,256]{2,1,0:T(2,128)} %shard_map.60), calls=%async_computation.1 | async-start | bytes 262144 | tf_op jit(solution)/shard_map/all_to_all | solution.py:476
  61.8 1.3 %copy-done.3 = bf16[2304,256]{1,0:T(8,128)(2,1)S(1)} copy-done((bf16[2304,256]{1,0:T(8,128)(2,1)S(1)}, bf16[2304,256]{1,0:T(8,128)(2,1)}, u32[]{:S(2)}) %copy-start.3) | copy-done | bytes 1179672
  63.0 7.8 %shard_map.61 = (bf16[22,48,2304]{2,1,0:T(8,128)(2,1)}, bf16[9,256,256]{2,1,0:T(8,128)(2,1)S(1)}) custom-call(f32[1,256]{1,0:T(1,128)S(1)} %get-tuple-element.31.mean_ref.local_mean_ref, f32[24,256]{1,0:T(8,128)S(1)} %get-tuple-element.32.shift_ref, bf16[22,64,256]{2,1,0:T(8,128)(2,1)S(1)} %get-tuple-element.33.mid_ref, bf16[2304,256]{1,0:T(8,128)(2,1)S(1)} %copy-done.3, ...), custom_call_target="tpu_custom_call" | custom-call | flops 8999999488 | bytes 1000000 | tf_op jit(solution)/shard_map/pallas_call | solution.py:461
  70.8 2.6 %all-to-all-done.1.gathered_ref = f32[64,2,256]{2,1,0:T(2,128)S(1)} async-done(((f32[64,2,256]{2,1,0:T(2,128)}), f32[64,2,256]{2,1,0:T(2,128)S(1)}, u32[]{:S(2)}, u32[]{:S(2)}) %all-to-all-start.1) | async-done | bytes 131104 | tf_op jit(solution)/shard_map/all_to_all | solution.py:476
  73.4 5.7 %shard_map.62 = bf16[22,44,256]{2,1,0:T(8,128)(2,1)} custom-call(f32[64,2,256]{2,1,0:T(2,128)S(1)} %all-to-all-done.1.gathered_ref, f32[1,256]{1,0:T(1,128)S(1)} %get-tuple-element.31.mean_ref.local_mean_ref, bf16[9,256,256]{2,1,0:T(8,128)(2,1)S(1)} %get-tuple-element.38.mix_ref, bf16[22,64,256]{2,1,0:T(8,128)(2,1)S(1)} %get-tuple-element.33.mid_ref, ...), custom_call_target="tpu_custom_call" | custom-call | flops 2000000000 | bytes 1000000 | tf_op jit(solution)/shard_map/pallas_call | solution.py:461
  (8 shorter events, 0.0 us)
Async XLA Ops:
  0.0 19.8 %collective-permute-start.1 = (bf16[22,44,256]{2,1,0:T(8,128)(2,1)}, bf16[22,44,256]{2,1,0:T(8,128)(2,1)S(1)}, u32[]{:S(2)}, u32[]{:S(2)}) collective-permute-start(bf16[22,44,256]{2,1,0:T(8,128)(2,1)} %own_any.3), channel_id=1, source_target_pairs={{0,1},{1,0},{2,3},{3,2},{4,5},{5,4},{6,7},{7,6},{8,9},{9,8},{10,11... | collective-permute-start | bytes 1486856 | tf_op jit(solution)/shard_map/ppermute | solution.py:472
  3.2 16.5 %collective-permute-start = (bf16[22,44,256]{2,1,0:T(8,128)(2,1)}, bf16[22,44,256]{2,1,0:T(8,128)(2,1)S(1)}, u32[]{:S(2)}, u32[]{:S(2)}) collective-permute-start(bf16[22,44,256]{2,1,0:T(8,128)(2,1)} %own_any.3), channel_id=1, source_target_pairs={{1,2},{2,1},{3,4},{4,3},{5,6},{6,5},{7,8},{8,7},{9,10},{10,9},{11,... | collective-permute-start | bytes 1486856 | tf_op jit(solution)/shard_map/ppermute | solution.py:504
  4.7 5.1 %collective-permute-start.2 = (f32[2,256]{1,0:T(2,128)S(1)}, f32[2,256]{1,0:T(2,128)S(1)}, u32[]{:S(2)}, u32[]{:S(2)}) collective-permute-start(f32[2,256]{1,0:T(2,128)S(1)} %get-tuple-element.25.sums_ref), channel_id=1, source_target_pairs={{0,1},{1,0},{2,3},{3,2},{4,5},{5,4},{6,7},{7,6},{8,9},{9,8},{10,11... | collective-permute-start | bytes 6152 | tf_op jit(solution)/shard_map/ppermute | solution.py:472
  10.5 23.1 %all-to-all-start = ((f32[64,2,256]{2,1,0:T(2,128)}), f32[64,2,256]{2,1,0:T(2,128)S(1)}, u32[]{:S(2)}, u32[]{:S(2)}) async-start(f32[64,2,256]{2,1,0:T(2,128)} %shard_map.56.both_ref), calls=%async_computation | async-start | bytes 262144 | tf_op jit(solution)/shard_map/all_to_all | solution.py:476
  19.8 13.7 %copy-start = (bf16[22,44,256]{2,1,0:T(8,128)(2,1)}, bf16[22,44,256]{2,1,0:T(8,128)(2,1)S(1)}, u32[]{:S(2)}) copy-start(bf16[22,44,256]{2,1,0:T(8,128)(2,1)S(1)} %collective-permute-done.1.core_ref.core_any) | copy-start | bytes 1486852
  19.8 13.7 %copy-start.1 = (bf16[22,44,256]{2,1,0:T(8,128)(2,1)}, bf16[22,44,256]{2,1,0:T(8,128)(2,1)S(1)}, u32[]{:S(2)}) copy-start(bf16[22,44,256]{2,1,0:T(8,128)(2,1)S(1)} %collective-permute-done.z_ref.z_any) | copy-start | bytes 1486852
  21.7 11.8 %collective-permute-start.4 = (bf16[7,44,256]{2,1,0:T(8,128)(2,1)S(1)}, bf16[7,44,256]{2,1,0:T(8,128)(2,1)S(1)}, u32[]{:S(2)}, u32[]{:S(2)}) collective-permute-start(bf16[7,44,256]{2,1,0:T(8,128)(2,1)S(1)} %get-tuple-element.27), channel_id=1, source_target_pairs={{16,32},{32,16},{48,64},{64,48},{80,96},{96,80},{17,33},{33,17},{4... | collective-permute-start | bytes 473096 | tf_op jit(solution)/shard_map/ppermute | solution.py:538
  22.4 12.7 %collective-permute-start.3 = (bf16[7,44,256]{2,1,0:T(8,128)(2,1)S(1)}, bf16[7,44,256]{2,1,0:T(8,128)(2,1)S(1)}, u32[]{:S(2)}, u32[]{:S(2)}) collective-permute-start(bf16[7,44,256]{2,1,0:T(8,128)(2,1)S(1)} %get-tuple-element.26.message_ref), channel_id=1, source_target_pairs={{0,16},{16,0},{32,48},{48,32},{64,80},{80,64},{96,112},{112,96},{1... | collective-permute-start | bytes 473096 | tf_op jit(solution)/shard_map/ppermute | solution.py:537
  46.3 1.0 %copy-start.2 = (bf16[2304,256]{1,0:T(8,128)(2,1)}, bf16[2304,256]{1,0:T(8,128)(2,1)S(1)}, u32[]{:S(2)}) copy-start(bf16[2304,256]{1,0:T(8,128)(2,1)S(1)} %get-tuple-element.34.scaled_ref) | copy-start | bytes 3538948
  47.4 2.3 %collective-permute-start.5 = (f32[2,256]{1,0:T(2,128)S(1)}, f32[2,256]{1,0:T(2,128)S(1)}, u32[]{:S(2)}, u32[]{:S(2)}) collective-permute-start(f32[2,256]{1,0:T(2,128)S(1)} %get-tuple-element.30.sums_ref), channel_id=1, source_target_pairs={{0,1},{1,0},{2,3},{3,2},{4,5},{5,4},{6,7},{7,6},{8,9},{9,8},{10,11... | collective-permute-start | bytes 6152 | tf_op jit(solution)/shard_map/ppermute | solution.py:472
  50.3 23.0 %all-to-all-start.1 = ((f32[64,2,256]{2,1,0:T(2,128)}), f32[64,2,256]{2,1,0:T(2,128)S(1)}, u32[]{:S(2)}, u32[]{:S(2)}) async-start(f32[64,2,256]{2,1,0:T(2,128)} %shard_map.60), calls=%async_computation.1 | async-start | bytes 262144 | tf_op jit(solution)/shard_map/all_to_all | solution.py:476
  61.8 1.3 %copy-start.3 = (bf16[2304,256]{1,0:T(8,128)(2,1)S(1)}, bf16[2304,256]{1,0:T(8,128)(2,1)}, u32[]{:S(2)}) copy-start(bf16[2304,256]{1,0:T(8,128)(2,1)} %copy-done.2) | copy-start | bytes 3538948

commit v5 on v3

--- a/solution.py
+++ b/solution.py
@@ -338,16 +338,17 @@
     mean_ref, shift_ref, mid_ref, res_any, band_any, scaled_any, s_any, mix_any,
     out_any, mix_ref, res_ref, u_ref, s_ref, rows_ref, out_ref, scaled_ref, band_ref, in_sems, out_sems,
 ):
-    *fetches, band_in, mix_in = start_all(
-        [(scaled_any, scaled_ref), (res_any, res_ref)]
-        + [
-            (s_any.at[pl.ds(1, ROWS), pl.ds(n * (WIDE - TILE), TILE)], s_ref.at[n])
-            for n in range(2)
-        ]
-        + [(s_any.at[n * (ROWS + 1)], rows_ref.at[n]) for n in range(2)]
-        + [(band_any, band_ref), (mix_any.at[1], mix_ref)],
+    strips = [(pl.ds(1, ROWS), pl.ds(n * (WIDE - TILE), TILE)) for n in range(2)]
+    edges = [n * (ROWS + 1) for n in range(2)]
+    fetches = start_all(
+        [(scaled_any, scaled_ref)]
+        + [(s_any.at[at], s_ref.at[n]) for n, at in enumerate(strips)]
+        + [(s_any.at[at], rows_ref.at[n]) for n, at in enumerate(edges)]
+        + [(res_any.at[at], res_ref.at[at]) for at in strips + edges],
         in_sems,
     )
+    band_in = pltpu.make_async_copy(band_any, band_ref, in_sems.at[9])
+    mix_in = pltpu.make_async_copy(mix_any.at[1], mix_ref, in_sems.at[10])
     local_mean = mean_ref[...]
 
     def mid_row(i, _):
@@ -358,6 +359,8 @@
 
     for fetch in fetches:
         fetch.wait()
+    band_in.start()
+    mix_in.start()
     for left in range(2):
         at = slice(left * (WIDE - TILE), left * (WIDE - TILE) + TILE)
         lhs = s_ref[left].reshape(ROWS * TILE, DEEP)
@@ -582,7 +585,7 @@
             buffer(ROWS, own_cols, DEEP),
             buffer(DEEP, CHANS),
             buffer(ROWS, HIGH, 4 * SPAN),
-            semaphores(8),
+            semaphores(11),
             semaphores(11),
         ],
         flops=9 * 10**9,

time: 77.9 us -> 77.9 us (level)
  transfers between devices with their start and end apart: 8 -> 8, of which waited for: 4 -> 4; matrix products, arithmetic and copies ran while one was open for 0% -> 0% of each run, Pallas kernels for 24% -> 23%
where the time goes in v5:
time: 77.9 us; the launch traced here: 77.5 us
  starting transfers between devices  35.5 us (46%)
  Pallas kernels  35.1 us (45%)
  waiting for transfers between devices  6.66 us (9%)
    pallas_call x8, Pallas kernels, call(): run(*[in_place(v, spec) for v, spec in zip(values, ins)])  35.1 us
    all_to_all x2, starting transfers between devices, gather(): return lax.all_to_all(both, ('y', 'xh', 'z'), 0, 0)  20.7 us
    ppermute x3, starting transfers between devices, from_other_core(): return lax.ppermute(v, 'core', [(0, 1), (1, 0)])  9.12 us
    ppermute x1, starting transfers between devices, local(): got_a = lax.ppermute(to_a, LAT, swap_pairs(8, 0))  5.03 us
    all_to_all x2, waiting for transfers between devices, gather(): return lax.all_to_all(both, ('y', 'xh', 'z'), 0, 0)  3.51 us
    ppermute x3, waiting for transfers between devices, from_other_core(): return lax.ppermute(v, 'core', [(0, 1), (1, 0)])  1.64 us
  transfers between devices with their start and end apart: 8, of which 4 were waited for; matrix products, arithmetic and copies ran while one was open for 0% of the time, Pallas kernels for 23%

profile of v5, /device:TPU:1, one launch (start us, length us, event | category | flops | bytes accessed | tf_op | source)
XLA Modules:
  0.0 77.5 jit_solution(12377820895453183274)
XLA Ops:
  0.0 3.2 %collective-permute-start.1 = (bf16[22,44,256]{2,1,0:T(8,128)(2,1)}, bf16[22,44,256]{2,1,0:T(8,128)(2,1)S(1)}, u32[]{:S(2)}, u32[]{:S(2)}) collective-permute-start(bf16[22,44,256]{2,1,0:T(8,128)(2,1)} %own_any.3), channel_id=1, source_target_pairs={{0,1},{1,0},{2,3},{3,2},{4,5},{5,4},{6,7},{7,6},{8,9},{9,8},{10,11... | collective-permute-start | bytes 1486856 | tf_op jit(solution)/shard_map/ppermute | solution.py:475
  3.2 0.0 collective-permute-start
  3.2 1.4 %shard_map.55 = (f32[2,256]{1,0:T(2,128)S(1)}, f32[1,256]{1,0:T(1,128)S(1)}, f32[2,27,128]{2,1,0:T(8,128)S(1)}) custom-call(bf16[22,44,256]{2,1,0:T(8,128)(2,1)} %own_any.3, s32[22]{0:T(128)} %reach_any.3, bf16[9,22,3,2,45]{4,3,2,1,0:T(2,128)(2,1)} %bitcast.1), custom_call_target="tpu_custom_call" | custom-call | flops 1000000 | bytes 1000000 | tf_op jit(solution)/shard_map/pallas_call | solution.py:464
  4.7 4.3 %collective-permute-start.2 = (f32[2,256]{1,0:T(2,128)S(1)}, f32[2,256]{1,0:T(2,128)S(1)}, u32[]{:S(2)}, u32[]{:S(2)}) collective-permute-start(f32[2,256]{1,0:T(2,128)S(1)} %get-tuple-element.25.sums_ref), channel_id=1, source_target_pairs={{0,1},{1,0},{2,3},{3,2},{4,5},{5,4},{6,7},{7,6},{8,9},{9,8},{10,11... | collective-permute-start | bytes 6152 | tf_op jit(solution)/shard_map/ppermute | solution.py:475
  9.0 0.8 %collective-permute-done.2.other_ref = f32[2,256]{1,0:T(2,128)S(1)} collective-permute-done((f32[2,256]{1,0:T(2,128)S(1)}, f32[2,256]{1,0:T(2,128)S(1)}, u32[]{:S(2)}, u32[]{:S(2)}) %collective-permute-start.2) | collective-permute-done | bytes 2080 | tf_op jit(solution)/shard_map/ppermute | solution.py:475
  9.8 0.7 shard_map.56.both_ref
  10.5 9.3 %all-to-all-start = ((f32[64,2,256]{2,1,0:T(2,128)}), f32[64,2,256]{2,1,0:T(2,128)S(1)}, u32[]{:S(2)}, u32[]{:S(2)}) async-start(f32[64,2,256]{2,1,0:T(2,128)} %shard_map.56.both_ref), calls=%async_computation | async-start | bytes 262144 | tf_op jit(solution)/shard_map/all_to_all | solution.py:479
  19.8 0.0 collective-permute-done.1.core_ref.core_any
  19.8 0.0 collective-permute-done.z_ref.z_any
  19.8 0.0 copy-start.1
  19.8 1.9 %shard_map.57 = (bf16[7,44,256]{2,1,0:T(8,128)(2,1)S(1)}, bf16[7,44,256]{2,1,0:T(8,128)(2,1)S(1)}) custom-call(bf16[22,44,256]{2,1,0:T(8,128)(2,1)S(1)} %collective-permute-done.z_ref.z_any, bf16[22,44,256]{2,1,0:T(8,128)(2,1)} %own_any.3, bf16[22,44,256]{2,1,0:T(8,128)(2,1)S(1)} %collective-permute-done.1.core_ref.core_any, ...), custom_call_target="tpu_custom_call" | custom-call | flops 1000000 | bytes 1000000 | tf_op jit(solution)/shard_map/pallas_call | solution.py:464
  21.7 0.7 collective-permute-start.4
  22.4 5.0 %collective-permute-start.3 = (bf16[7,44,256]{2,1,0:T(8,128)(2,1)S(1)}, bf16[7,44,256]{2,1,0:T(8,128)(2,1)S(1)}, u32[]{:S(2)}, u32[]{:S(2)}) collective-permute-start(bf16[7,44,256]{2,1,0:T(8,128)(2,1)S(1)} %get-tuple-element.26.message_ref), channel_id=1, source_target_pairs={{0,16},{16,0},{32,48},{48,32},{64,80},{80,64},{96,112},{112,96},{1... | collective-permute-start | bytes 473096 | tf_op jit(solution)/shard_map/ppermute | solution.py:540
  27.4 6.1 %shard_map.58 = (bf16[22,144,256]{2,1,0:T(8,128)(2,1)}, f32[22,2304]{1,0:T(8,128)}, bf16[22,144,256]{2,1,0:T(8,128)(2,1)}, f32[22,2304]{1,0:T(8,128)}) custom-call(bf16[7,44,256]{2,1,0:T(8,128)(2,1)S(1)} %get-tuple-element.26.message_ref, s32[22]{0:T(128)} %reach_any.3, bf16[9,22,3,2,45]{4,3,2,1,0:T(2,128)(2,1)} %bitcast.2), custom_call_target="tpu_custom_call" | custom-call | flops 5000000000 | bytes 1000000 | tf_op jit(solution)/shard_map/pallas_call | solution.py:464
  33.6 0.0 all-to-all-done.gathered_ref
  33.6 1.5 %collective-permute-done.3.a_ref = bf16[7,44,256]{2,1,0:T(8,128)(2,1)S(1)} collective-permute-done((bf16[7,44,256]{2,1,0:T(8,128)(2,1)S(1)}, bf16[7,44,256]{2,1,0:T(8,128)(2,1)S(1)}, u32[]{:S(2)}, u32[]{:S(2)}) %collective-permute-start.3) | collective-permute-done | bytes 157728 | tf_op jit(solution)/shard_map/ppermute | solution.py:540
  35.1 10.5 %shard_map.59 = (bf16[24,96,2304]{2,1,0:T(8,128)(2,1)}, bf16[24,96,256]{2,1,0:T(8,128)(2,1)}, bf16[22,64,256]{2,1,0:T(8,128)(2,1)S(1)}, f32[24,256]{1,0:T(8,128)...) custom-call(f32[1,256]{1,0:T(1,128)S(1)} %get-tuple-element.23.local_mean_ref, ...), custom_call_target="tpu_custom_call" | custom-call | flops 1000000 | bytes 1000000 | tf_op jit(solution)/shard_map/pallas_call | solution.py:464
  45.6 1.6 %collective-permute-start.5 = (f32[2,256]{1,0:T(2,128)S(1)}, f32[2,256]{1,0:T(2,128)S(1)}, u32[]{:S(2)}, u32[]{:S(2)}) collective-permute-start(f32[2,256]{1,0:T(2,128)S(1)} %get-tuple-element.30.sums_ref), channel_id=1, source_target_pairs={{0,1},{1,0},{2,3},{3,2},{4,5},{5,4},{6,7},{7,6},{8,9},{9,8},{10,11... | collective-permute-start | bytes 6152 | tf_op jit(solution)/shard_map/ppermute | solution.py:475
  47.2 0.8 %collective-permute-done.5.other_ref = f32[2,256]{1,0:T(2,128)S(1)} collective-permute-done((f32[2,256]{1,0:T(2,128)S(1)}, f32[2,256]{1,0:T(2,128)S(1)}, u32[]{:S(2)}, u32[]{:S(2)}) %collective-permute-start.5) | collective-permute-done | bytes 2080 | tf_op jit(solution)/shard_map/ppermute | solution.py:475
  48.0 0.7 shard_map.60
  48.7 11.4 %all-to-all-start.1 = ((f32[64,2,256]{2,1,0:T(2,128)}), f32[64,2,256]{2,1,0:T(2,128)S(1)}, u32[]{:S(2)}, u32[]{:S(2)}) async-start(f32[64,2,256]{2,1,0:T(2,128)} %shard_map.60), calls=%async_computation.1 | async-start | bytes 262144 | tf_op jit(solution)/shard_map/all_to_all | solution.py:479
  60.1 8.1 %shard_map.61 = (bf16[22,48,2304]{2,1,0:T(8,128)(2,1)}, bf16[9,256,256]{2,1,0:T(8,128)(2,1)S(1)}) custom-call(f32[1,256]{1,0:T(1,128)S(1)} %get-tuple-element.31.mean_ref.local_mean_ref, f32[24,256]{1,0:T(8,128)S(1)} %get-tuple-element.32.shift_ref, bf16[22,64,256]{2,1,0:T(8,128)(2,1)S(1)} %get-tuple-element.33.mid_ref, ...), custom_call_target="tpu_custom_call" | custom-call | flops 8999999488 | bytes 1000000 | tf_op jit(solution)/shard_map/pallas_call | solution.py:464
  68.2 3.5 %all-to-all-done.1.gathered_ref = f32[64,2,256]{2,1,0:T(2,128)S(1)} async-done(((f32[64,2,256]{2,1,0:T(2,128)}), f32[64,2,256]{2,1,0:T(2,128)S(1)}, u32[]{:S(2)}, u32[]{:S(2)}) %all-to-all-start.1) | async-done | bytes 131104 | tf_op jit(solution)/shard_map/all_to_all | solution.py:479
  71.7 5.7 %shard_map.62 = bf16[22,44,256]{2,1,0:T(8,128)(2,1)} custom-call(f32[64,2,256]{2,1,0:T(2,128)S(1)} %all-to-all-done.1.gathered_ref, f32[1,256]{1,0:T(1,128)S(1)} %get-tuple-element.31.mean_ref.local_mean_ref, bf16[9,256,256]{2,1,0:T(8,128)(2,1)S(1)} %get-tuple-element.38.mix_ref, bf16[22,64,256]{2,1,0:T(8,128)(2,1)S(1)} %get-tuple-element.33.mid_ref, ...), custom_call_target="tpu_custom_call" | custom-call | flops 2000000000 | bytes 1000000 | tf_op jit(solution)/shard_map/pallas_call | solution.py:464
  (4 shorter events, 0.0 us)
Async XLA Ops:
  0.0 19.8 %collective-permute-start.1 = (bf16[22,44,256]{2,1,0:T(8,128)(2,1)}, bf16[22,44,256]{2,1,0:T(8,128)(2,1)S(1)}, u32[]{:S(2)}, u32[]{:S(2)}) collective-permute-start(bf16[22,44,256]{2,1,0:T(8,128)(2,1)} %own_any.3), channel_id=1, source_target_pairs={{0,1},{1,0},{2,3},{3,2},{4,5},{5,4},{6,7},{7,6},{8,9},{9,8},{10,11... | collective-permute-start | bytes 1486856 | tf_op jit(solution)/shard_map/ppermute | solution.py:475
  3.2 16.6 %collective-permute-start = (bf16[22,44,256]{2,1,0:T(8,128)(2,1)}, bf16[22,44,256]{2,1,0:T(8,128)(2,1)S(1)}, u32[]{:S(2)}, u32[]{:S(2)}) collective-permute-start(bf16[22,44,256]{2,1,0:T(8,128)(2,1)} %own_any.3), channel_id=1, source_target_pairs={{1,2},{2,1},{3,4},{4,3},{5,6},{6,5},{7,8},{8,7},{9,10},{10,9},{11,... | collective-permute-start | bytes 1486856 | tf_op jit(solution)/shard_map/ppermute | solution.py:507
  4.7 5.1 %collective-permute-start.2 = (f32[2,256]{1,0:T(2,128)S(1)}, f32[2,256]{1,0:T(2,128)S(1)}, u32[]{:S(2)}, u32[]{:S(2)}) collective-permute-start(f32[2,256]{1,0:T(2,128)S(1)} %get-tuple-element.25.sums_ref), channel_id=1, source_target_pairs={{0,1},{1,0},{2,3},{3,2},{4,5},{5,4},{6,7},{7,6},{8,9},{9,8},{10,11... | collective-permute-start | bytes 6152 | tf_op jit(solution)/shard_map/ppermute | solution.py:475
  10.5 23.1 %all-to-all-start = ((f32[64,2,256]{2,1,0:T(2,128)}), f32[64,2,256]{2,1,0:T(2,128)S(1)}, u32[]{:S(2)}, u32[]{:S(2)}) async-start(f32[64,2,256]{2,1,0:T(2,128)} %shard_map.56.both_ref), calls=%async_computation | async-start | bytes 262144 | tf_op jit(solution)/shard_map/all_to_all | solution.py:479
  19.8 13.8 %copy-start = (bf16[22,44,256]{2,1,0:T(8,128)(2,1)}, bf16[22,44,256]{2,1,0:T(8,128)(2,1)S(1)}, u32[]{:S(2)}) copy-start(bf16[22,44,256]{2,1,0:T(8,128)(2,1)S(1)} %collective-permute-done.1.core_ref.core_any) | copy-start | bytes 1486852
  19.8 13.8 %copy-start.1 = (bf16[22,44,256]{2,1,0:T(8,128)(2,1)}, bf16[22,44,256]{2,1,0:T(8,128)(2,1)S(1)}, u32[]{:S(2)}) copy-start(bf16[22,44,256]{2,1,0:T(8,128)(2,1)S(1)} %collective-permute-done.z_ref.z_any) | copy-start | bytes 1486852
  21.7 11.9 %collective-permute-start.4 = (bf16[7,44,256]{2,1,0:T(8,128)(2,1)S(1)}, bf16[7,44,256]{2,1,0:T(8,128)(2,1)S(1)}, u32[]{:S(2)}, u32[]{:S(2)}) collective-permute-start(bf16[7,44,256]{2,1,0:T(8,128)(2,1)S(1)} %get-tuple-element.27), channel_id=1, source_target_pairs={{16,32},{32,16},{48,64},{64,48},{80,96},{96,80},{17,33},{33,17},{4... | collective-permute-start | bytes 473096 | tf_op jit(solution)/shard_map/ppermute | solution.py:541
  22.4 12.7 %collective-permute-start.3 = (bf16[7,44,256]{2,1,0:T(8,128)(2,1)S(1)}, bf16[7,44,256]{2,1,0:T(8,128)(2,1)S(1)}, u32[]{:S(2)}, u32[]{:S(2)}) collective-permute-start(bf16[7,44,256]{2,1,0:T(8,128)(2,1)S(1)} %get-tuple-element.26.message_ref), channel_id=1, source_target_pairs={{0,16},{16,0},{32,48},{48,32},{64,80},{80,64},{96,112},{112,96},{1... | collective-permute-start | bytes 473096 | tf_op jit(solution)/shard_map/ppermute | solution.py:540
  45.6 2.4 %collective-permute-start.5 = (f32[2,256]{1,0:T(2,128)S(1)}, f32[2,256]{1,0:T(2,128)S(1)}, u32[]{:S(2)}, u32[]{:S(2)}) collective-permute-start(f32[2,256]{1,0:T(2,128)S(1)} %get-tuple-element.30.sums_ref), channel_id=1, source_target_pairs={{0,1},{1,0},{2,3},{3,2},{4,5},{5,4},{6,7},{7,6},{8,9},{9,8},{10,11... | collective-permute-start | bytes 6152 | tf_op jit(solution)/shard_map/ppermute | solution.py:475
  48.7 23.0 %all-to-all-start.1 = ((f32[64,2,256]{2,1,0:T(2,128)}), f32[64,2,256]{2,1,0:T(2,128)S(1)}, u32[]{:S(2)}, u32[]{:S(2)}) async-start(f32[64,2,256]{2,1,0:T(2,128)} %shard_map.60), calls=%async_computation.1 | async-start | bytes 262144 | tf_op jit(solution)/shard_map/all_to_all | solution.py:479
